TPU v7x, 256 devices: a whole 4x4x8 slice. The times are simulated.
256 devices in a mesh: rows: 4 (over y_lo, core), gr: 8 (over x, y_hi), gc: 8 (over z).
Axes of the slice: x: 4, y: 4 (y_hi: 2, y_lo: 2; y = y_hi * 2 + y_lo), z: 8, core: 2. Of those that a mesh axis runs over, the one named last changes fastest.
Arguments:
- samples: float32 [2048, 8192], P(('rows', 'gc'), 'gr'), may hold values from -6 to 6
- targets: float32 [2048], P(('rows', 'gc')), may hold values from -6 to 6
- ridge: float32 [8192], P('gr'), may hold values from 0.5 to 2
Outputs:
- trailing: float32 [8192, 8192], P('gr', 'gc')
- panel: float32 [8192, 512], P('gr')
- reduced_rhs: float32 [8192], P('gr')
All inputs are finite; a program needn't handle non-finite values.
Results may differ from a plain program's by a relative error of at most 0.00011.
Values sent between devices are 32-bit elements; how exact they have to be, the bound alone decides.
A program may use at most 64 MiB of HBM per device.

v0:
```python
import jax
import jax.numpy as jnp
from jax import lax
from jax.sharding import PartitionSpec as P

PANEL = 512


def broadcast(value, axis, source):
    kept = jnp.where(lax.axis_index(axis) == source, value, 0).astype(value.dtype)
    return lax.psum(kept, axis)


def add_ridge(block, ridge_rows, row_start, col_start):
    row_ids = row_start + jnp.arange(block.shape[0])[:, None]
    col_ids = col_start + jnp.arange(block.shape[1])[None, :]
    return block + jnp.where(row_ids == col_ids, ridge_rows[:, None], 0.0)


def on_device(samples, targets, ridge):
    highest = lax.Precision.HIGHEST
    n_rows = lax.axis_size("rows")
    n_gr = lax.axis_size("gr")
    n_gc = lax.axis_size("gc")
    row_width = samples.shape[1]
    col_width = row_width * n_gr // n_gc
    row_block = lax.axis_index("gr")
    col_block = lax.axis_index("gc")
    owner = col_block * col_width // row_width
    left, labels = (
        lax.all_gather(samples, "gc", axis=0, tiled=True),
        lax.all_gather(targets, "gc", axis=0, tiled=True),
    )
    count = left.shape[0] * n_rows
    right = broadcast(left, "gr", owner)
    partial_value = lax.dot_general(
        left, right, (((0,), (0,)), ((), ())), precision=highest, preferred_element_type=jnp.float32
    )
    partial_rhs = jnp.dot(labels, left, precision=highest, preferred_element_type=jnp.float32)
    share = row_width // n_rows
    share_start = lax.axis_index("rows") * share
    summed, rhs_share = (
        lax.psum_scatter(partial_value, "rows", scatter_dimension=0, tiled=True),
        lax.psum_scatter(partial_rhs, "rows", scatter_dimension=0, tiled=True),
    )
    ridge_share = lax.dynamic_slice_in_dim(ridge, share_start, share, 0)
    tile = add_ridge(
        summed / count, ridge_share, row_block * row_width + share_start, col_block * col_width
    )
    cols_share = broadcast(tile[:, :PANEL], "gc", 0)
    panel_cols, rhs = (
        lax.all_gather(cols_share, "rows", axis=0, tiled=True),
        lax.all_gather(rhs_share / count, "rows", axis=0, tiled=True),
    )
    diag_block, rhs_top = (broadcast(panel_cols[:PANEL], "gr", 0), broadcast(rhs[:PANEL], "gr", 0))
    top = jnp.linalg.cholesky(diag_block)
    panel = jax.scipy.linalg.solve_triangular(top, panel_cols.T, lower=True).T
    col_factor = broadcast(panel, "gr", owner)
    panel_share = lax.dynamic_slice_in_dim(panel, share_start, share, 0)
    updated = tile - jnp.dot(
        panel_share, col_factor.T, precision=highest, preferred_element_type=jnp.float32
    )
    trailing = lax.all_gather(updated, "rows", axis=0, tiled=True)
    solved = jax.scipy.linalg.solve_triangular(top, rhs_top, lower=True)
    reduced_rhs = rhs - jnp.dot(
        panel, solved, precision=highest, preferred_element_type=jnp.float32
    )
    return (trailing, panel, reduced_rhs)


def solution(mesh):
    in_specs = (P(("rows", "gc"), "gr"), P(("rows", "gc")), P("gr"))
    out_specs = (P("gr", "gc"), P("gr", None), P("gr"))
    return jax.shard_map(
        on_device, mesh=mesh, in_specs=in_specs, out_specs=out_specs, check_vma=False
    )
```

profile of v0, /device:TPU:1, one launch (start us, length us, event | category | flops | bytes accessed | tf_op | source)
XLA Modules:
  0.0 794.7 jit_solution(1955744989832727800)
XLA Ops:
  8.0 43.1 %all-gather.5.cloned.1.call-done = f32[512,1024]{1,0:T(8,128)} async-done(((f32[64,1024]{1,0:T(8,128)}), f32[512,1024]{1,0:T(8,128)}) %all-gather.5.cloned.1.call-update) | async-done | bytes 2097168 | tf_op jit(solution)/shard_map/all_gather | solution.py:31
  54.3 114.1 %all-reduce.8.cloned.1.call-done = f32[512,1024]{1,0:T(8,128)} async-done(((f32[512,1024]{1,0:T(8,128)}), f32[512,1024]{1,0:T(8,128)}) %all-reduce.8.cloned.1.call-update) | async-done | bytes 2097168 | tf_op jit(solution)/shard_map/psum | solution.py:11
  168.4 9.5 %convolution_bitcast_fusion = f32[1024,1024]{0,1:T(8,128)} fusion(f32[512,1024]{1,0:T(8,128)} %all-reduce.8.cloned.1.call-done, f32[512,1024]{1,0:T(8,128)S(1)} %copy-done), kind=kOutput, calls=%fused_computation.2 | convolution fusion | flops 6442450944 | bytes 8388608 | tf_op jit(solution)/shard_map/dot_general | solution.py:36
  178.8 50.7 %reduce-scatter.2.cloned.1.call-done = f32[256,1024]{0,1:T(8,128)} async-done(((f32[1024,1024]{0,1:T(8,128)}), f32[256,1024]{0,1:T(8,128)}) %reduce-scatter.2.cloned.1.call-update) | async-done | bytes 1048592 | tf_op jit(solution)/shard_map/reduce_scatter | solution.py:43
  232.8 69.6 %all-reduce.10.cloned.1.call-done = f32[256,512]{0,1:T(8,128)} async-done(((f32[256,512]{0,1:T(8,128)}), f32[256,512]{0,1:T(8,128)}) %all-reduce.10.cloned.1.call-update) | async-done | bytes 524304 | tf_op jit(solution)/shard_map/psum | solution.py:11
  302.5 36.7 %all-gather.7.cloned.1.call-done = f32[1024,512]{0,1:T(8,128)} async-done(((f32[256,512]{0,1:T(8,128)}), f32[1024,512]{0,1:T(8,128)}) %all-gather.7.cloned.1.call-update) | async-done | bytes 2097168 | tf_op jit(solution)/shard_map/all_gather | solution.py:52
  341.7 90.0 %all-reduce.12.cloned.1.call-done = f32[512,512]{0,1:T(8,128)} async-done(((f32[512,512]{0,1:T(8,128)}), f32[512,512]{0,1:T(8,128)}) %all-reduce.12.cloned.1.call-update) | async-done | bytes 1048592 | tf_op jit(solution)/shard_map/psum | solution.py:11
  436.8 11.7 %cholesky.103 = f32[128,128]{1,0:T(8,128)S(1)} custom-call(f32[128,128]{1,0:T(8,128)S(1)} %cholesky.263), custom_call_target="Cholesky" | custom-call | tf_op jit(solution)/shard_map/jit(cholesky)/cholesky | solution.py:56
  449.2 9.8 %custom-call.34 = f32[1,128,128]{1,2,0:T(8,128)S(1)} custom-call(f32[1,128,128]{2,1,0:T(8,128)S(1)} %get-tuple-element.42), custom_call_target="InvertDiagBlocksLowerTriangular" | custom-call | tf_op jit(solution)/shard_map/jit(cholesky)/cholesky | solution.py:56
  461.7 11.7 %cholesky.215 = f32[128,128]{1,0:T(8,128)S(1)} custom-call(f32[128,128]{1,0:T(8,128)S(1)} %cholesky.267), custom_call_target="Cholesky" | custom-call | tf_op jit(solution)/shard_map/jit(cholesky)/cholesky | solution.py:56
  474.2 10.6 %custom-call.35 = f32[1,128,128]{1,2,0:T(8,128)} custom-call(f32[1,128,128]{2,1,0:T(8,128)S(1)} %get-tuple-element.40), custom_call_target="InvertDiagBlocksLowerTriangular" | custom-call | tf_op jit(solution)/shard_map/jit(cholesky)/cholesky | solution.py:56
  489.3 11.7 %cholesky.236 = f32[128,128]{1,0:T(8,128)S(1)} custom-call(f32[128,128]{1,0:T(8,128)S(1)} %cholesky.272), custom_call_target="Cholesky" | custom-call | tf_op jit(solution)/shard_map/jit(cholesky)/cholesky | solution.py:56
  501.1 9.8 %custom-call.36 = f32[1,128,128]{1,2,0:T(8,128)S(1)} custom-call(f32[1,128,128]{2,1,0:T(8,128)S(1)} %get-tuple-element.38), custom_call_target="InvertDiagBlocksLowerTriangular" | custom-call | tf_op jit(solution)/shard_map/jit(cholesky)/cholesky | solution.py:56
  512.6 12.1 %cholesky.253 = f32[128,128]{1,0:T(8,128)S(1)} custom-call(f32[128,128]{1,0:T(8,128)S(1)} %convolution_subtract_fusion.5), custom_call_target="Cholesky" | custom-call | tf_op jit(solution)/shard_map/jit(cholesky)/cholesky | solution.py:56
  530.4 14.3 %while.1 = (s32[]{:T(128)}, f32[512,512]{0,1:T(8,128)}, s32[4,2]{0,1:T(2,128)S(1)}, f32[4,128,128]{2,1,0:T(8,128)}, s32[]{:T(128)}) while((s32[]{:T(128)}, f32[512,512]{0,1:T(8,128)}, s32[4,2]{0,1:T(2,128)S(1)}, f32[4,128,128]{2,1,0:T(8,128)}, s32[]{:T(128)}) %tuple.32), condition=%wide.while_cond, body=%wide.while_body.sunk | while | flops 2 | bytes 393329 | solution.py:57
  544.8 40.1 %custom-call.37 = f32[4,128,128]{1,2,0:T(8,128)S(1)} custom-call(f32[4,128,128]{2,1,0:T(8,128)} %get-tuple-element.10), custom_call_target="InvertDiagBlocksLowerTriangular" | custom-call | tf_op jit(solution)/shard_map/jit(_solve_triangular)/triangular_solve | solution.py:57
  596.7 3.8 fusion.67
  600.5 111.3 %all-reduce.14.cloned.1.call-done = f32[1024,512]{0,1:T(8,128)} async-done(((f32[1024,512]{0,1:T(8,128)}), f32[1024,512]{0,1:T(8,128)}) %all-reduce.14.cloned.1.call-update) | async-done | bytes 2097168 | tf_op jit(solution)/shard_map/psum | solution.py:11
  711.8 6.5 convolution_subtract_fusion
  721.0 14.9 %all-reduce.1 = f32[512]{0:T(512)S(1)} all-reduce(f32[512]{0:T(512)S(1)} %dynamic-update-slice.23), channel_id=1, replica_groups=mesh['rows'=4,'gr'=8,'gc'=8] {'gc'}, use_global_device_ids=true, to_apply=%add.1 | all-reduce | flops 512 | bytes 4096
  737.1 11.3 %all-reduce.2 = f32[1024]{0:T(1024)S(1)} all-reduce(f32[1024]{0:T(1024)S(1)} %bitcast.122), channel_id=3, replica_groups=mesh['rows'=4,'gr'=8,'gc'=8] {'rows'}, use_global_device_ids=true, to_apply=%region_13.14.clone | all-reduce | flops 1024 | bytes 8192
  748.4 6.0 all-gather
  754.4 19.2 %psum.39 = f32[512]{0:T(512)S(1)} all-reduce(f32[512]{0:T(512)S(1)} %bitcast.124), channel_id=1, replica_groups=mesh['rows'=4,'gr'=8,'gc'=8] {'gr'}, use_global_device_ids=true, to_apply=%region_14.15 | all-reduce | flops 512 | bytes 4096 | tf_op jit(solution)/shard_map/psum | solution.py:11
  782.3 5.3 copy.28
  (125 shorter events, 66.7 us)
Async XLA Ops:
  7.2 43.9 %all-gather.5.cloned.1.call-start = ((), (), s32[]{:S(2)}) async-start(), calls=%async_computation.1 | async-start | bytes 2359296 | tf_op jit(solution)/shard_map/all_gather | solution.py:31
  7.9 160.5 %all-reduce.8.cloned.1.call-start = ((), (), s32[]{:S(2)}) async-start(), calls=%async_computation.2 | async-start | bytes 4194304 | tf_op jit(solution)/shard_map/psum | solution.py:11
  54.2 114.2 %copy-start = (f32[512,1024]{1,0:T(8,128)S(1)}, f32[512,1024]{1,0:T(8,128)}, u32[]{:S(2)}) copy-start(f32[512,1024]{1,0:T(8,128)} %all-gather.5.cloned.1.call-done) | copy-start | bytes 6291460
  54.3 175.2 %reduce-scatter.2.cloned.1.call-start = ((), (), s32[]{:S(2)}) async-start(), calls=%async_computation.3 | async-start | bytes 5242880 | tf_op jit(solution)/shard_map/reduce_scatter | solution.py:43
  178.0 124.5 %all-reduce.10.cloned.1.call-start = ((), (), s32[]{:S(2)}) async-start(), calls=%async_computation.4 | async-start | bytes 1048576 | tf_op jit(solution)/shard_map/psum | solution.py:11
  230.9 1.0 copy-start.3
  232.7 106.4 %all-gather.7.cloned.1.call-start = ((), (), s32[]{:S(2)}) async-start(), calls=%async_computation.5 | async-start | bytes 2621440 | tf_op jit(solution)/shard_map/all_gather | solution.py:52
  302.4 129.3 %all-reduce.12.cloned.1.call-start = ((), (), s32[]{:S(2)}) async-start(), calls=%async_computation.6 | async-start | bytes 2097152 | tf_op jit(solution)/shard_map/psum | solution.py:11
  341.5 370.3 %all-reduce.14.cloned.1.call-start = ((), (), s32[]{:S(2)}) async-start(), calls=%async_computation.7 | async-start | bytes 4194304 | tf_op jit(solution)/shard_map/psum | solution.py:11
  431.7 2.6 copy-start.7
  435.8 1.0 copy-start.8
  584.9 4.2 copy-start.6
  591.4 2.9 copy-start.1
  594.3 0.8 copy-start.4
  596.7 185.7 %all-gather.9.cloned.1.call-start = ((), (), s32[]{:S(2)}) async-start(), calls=%async_computation.8 | async-start | bytes 5242880 | tf_op jit(solution)/shard_map/all_gather | solution.py:63
  711.7 6.5 copy-start.11
  711.7 7.8 copy-start.10
  711.8 9.0 %copy-start.9 = (f32[64]{0:T(128)S(1)}, f32[64]{0:T(128)}, u32[]{:S(2)}) copy-start(f32[64]{0:T(128)} %param.4) | copy-start | bytes 772
  773.6 6.9 copy-start.2
  773.6 6.9 copy-start.5
Sparse Core Ops, SparseCore 0:
  9.8 41.1 all-gather.4
  54.4 113.9 all-reduce.7
  178.1 51.3 reduce-scatter.1
  232.8 69.5 all-reduce.9
  304.1 35.0 all-gather.6
  342.2 89.4 all-reduce.11
  596.8 114.9 all-reduce.13
  718.4 53.4 all-gather.8
where the time goes:
time: 800 us; the launch traced here: 795 us
  waiting for transfers between devices  516 us (64%)
  other arithmetic  136 us (17%)
  blocking collectives  51.4 us (6%)
  matrix products  38.3 us (5%)
  local copies, waits for them, and re-layouts  33.7 us (4%)
  between operations  18.5 us (2%)
    psum x4, waiting for transfers between devices, broadcast(): return lax.psum(kept, axis)  385 us
    another operation x14, other arithmetic, on_device(): top = jnp.linalg.cholesky(diag_block)  79.6 us
    reduce_scatter x1, waiting for transfers between devices, on_device(): lax.psum_scatter(partial_value, 'rows', scatter_dimension=0, tiled=True)  50.7 us
    all_gather x1, waiting for transfers between devices, on_device(): lax.all_gather(samples, 'gc', axis=0, tiled=True)  43.1 us
    another operation x3, other arithmetic, on_device(): panel = jax.scipy.linalg.solve_triangular(top, panel_cols.T, lower=True).T  41.3 us
    all_gather x1, waiting for transfers between devices, on_device(): lax.all_gather(cols_share, 'rows', axis=0, tiled=True)  36.7 us
    unnamed x2, blocking collectives  26.2 us
    psum x1, blocking collectives, broadcast(): return lax.psum(kept, axis)  19.2 us
  transfers between devices with their start and end apart: 8, of which 7 were waited for; matrix products, arithmetic and copies ran while one was open for 2% of the time, Pallas kernels for 0%

commit v1 on v0

v1 whole, which is shorter than its diff:
```python
import jax
import jax.numpy as jnp
from jax import lax
from jax.experimental import pallas as pl
from jax.experimental.pallas import tpu as pltpu
from jax.sharding import PartitionSpec as P

f32, bf16 = jnp.float32, jnp.bfloat16
MESH = pl.DeviceIdType.MESH
PANEL = 512
W = 1024
K = 2048
NZ = 8
N = 128


def fdot(a, b, dims=((1,), (0,))):
    return lax.dot_general(a, b, (dims, ((), ())), precision=lax.Precision.HIGHEST, preferred_element_type=f32)


def bdot(a, b, dims=((1,), (0,))):
    return lax.dot_general(a, b, (dims, ((), ())), preferred_element_type=f32)


def high_low(x):
    high = x.astype(bf16)
    return high, (x - high.astype(f32)).astype(bf16)


def split3(x):
    a = x.astype(bf16).astype(f32)
    r = x - a
    b = r.astype(bf16).astype(f32)
    return a, b, r - b


def stack_left(x):
    a, b, c = split3(x)
    return jnp.concatenate([a, a, a, b, b, c], 0).astype(bf16)


def stack_right(x):
    a, b, c = split3(x)
    return jnp.concatenate([a, b, c, a, b, a], 0).astype(bf16)


def dot3(a, b, dims):
    (da,), (db,) = dims
    ah, al = high_low(a)
    bh, bl = high_low(b)
    return bdot(jnp.concatenate([ah, al, ah], da), jnp.concatenate([bh, bh, bl], db), dims)


def row_of(x, i):
    return jnp.broadcast_to(x[i : i + 1, :], (8, x.shape[1]))


def twice(x):
    return jnp.concatenate([x, x], 1)


def strip_factor(s, strip):
    left = strip[:, :N]
    cols = [jnp.take_along_axis(left, jnp.full((8, N), s * 8 + j, jnp.int32), axis=1) for j in range(8)]
    e = {(i, j): row_of(cols[j], i) for j in range(8) for i in range(j, 8)}
    t = [row_of(strip, i) for i in range(8)]
    f, inv, root = {}, [], []
    for k in range(8):
        r = lax.rsqrt(e[k, k])
        r = r * (1.5 - 0.5 * e[k, k] * r * r)
        p = r * r
        p = p * (2.0 - e[k, k] * p)
        inv.append(p)
        root.append(r)
        for i in range(k + 1, 8):
            f[i, k] = e[i, k] * p
        for j in range(k + 1, 8):
            for i in range(j, 8):
                e[i, j] = e[i, j] - f[i, k] * e[j, k]
        for i in range(k + 1, 8):
            t[i] = t[i] - twice(f[i, k]) * t[k]
    y = [None] * 8
    for i in reversed(range(8)):
        acc = t[i] * twice(inv[i])
        for k in range(i + 1, 8):
            acc = acc - twice(f[k, i]) * y[k]
        y[i] = acc
    row = lax.broadcasted_iota(jnp.int32, (8, N), 0)

    def assemble(parts):
        out = parts[0]
        rows = row if out.shape[1] == N else twice(row)
        for i in range(1, 8):
            out = jnp.where(rows == i, parts[i], out)
        return out

    return assemble(y), assemble([t[i][:, N:] * root[i] for i in range(8)]), y


def factor_block(ab, m_ref):
    def body(s, carry):
        strip, left, right = carry
        ab[...] = ab[...] - bdot(left, right)
        whole, inverse_rows, y = strip_factor(s, strip)
        m_ref[pl.ds(pl.multiple_of(s * 8, 8), 8), :] = inverse_rows
        after = lax.rem(s + 1, 16)
        rows = ab[pl.ds(pl.multiple_of(after * 8, 8), 8), :]
        terms = []
        for j in range(8):
            c = jnp.take_along_axis(rows[:, :N], jnp.full((8, N), s * 8 + j, jnp.int32), axis=1)
            terms.append(twice(c) * y[j])
        while len(terms) > 1:
            terms = [terms[i] + terms[i + 1] for i in range(0, len(terms), 2)]
        return rows - terms[0], stack_left(strip[:, :N]).T, stack_right(whole)

    lax.fori_loop(0, 16, body, (ab[0:8, :], jnp.zeros((N, 48), bf16), jnp.zeros((48, 2 * N), bf16)))


def factor_inverse(a, b, ab, m):
    b[...] = jnp.zeros_like(b)
    eye = jnp.where(
        lax.broadcasted_iota(jnp.int32, (N, N), 0) == lax.broadcasted_iota(jnp.int32, (N, N), 1), 1.0, 0.0
    )
    blocks = PANEL // N
    for k in range(blocks):
        now, rest = slice(k * N, (k + 1) * N), slice((k + 1) * N, PANEL)
        ab[:, :N] = a[now, now]
        ab[:, N:] = eye
        factor_block(ab, m)
        b[now, now] = m[...]
        if k:
            b[now, : k * N] = fdot(m[...], b[now, : k * N])
        if k < blocks - 1:
            u = fdot(m[...], a[now, rest])
            a[rest, rest] = a[rest, rest] - fdot(u, u, ((0,), (0,)))
            b[rest, : (k + 1) * N] = b[rest, : (k + 1) * N] - fdot(u, b[now, : (k + 1) * N], ((0,), (0,)))


def gather_kernel(
    samp, targ, ridge,
    tpre_o, gi0_o, g0j_o, g00_o, rhs_o, top_o, ridge_o,
    chunk, ai, sj, zb, rg, ah, al, jh, jl, zh, zl, tpre, gi0, g0j, g00, rhs, top,
    ex_s, ex_r, ye_s, ye_r, si_s, si_r, sc_s, sc_r, zs_s, zs_r, rg_s, rg_r, zz_s, zz_r, ag_s, ag_r, d_s, d_r, o_s, o_r, lo,
):
    r, i, z = lax.axis_index("rows"), lax.axis_index("gr"), lax.axis_index("gc")
    core, yl = lax.rem(r, 2), r // 2
    x, yh = i // 2, lax.rem(i, 2)
    y = yh * 2 + yl
    p = y * 4 + x
    q = z * 2 + yl
    first, second = core == 0, core == 1

    def dev(xx, yy, zz, c):
        return {"rows": lax.rem(yy, 2) * 2 + c, "gr": xx * 2 + yy // 2, "gc": zz}

    def up(v, n):
        return lax.rem(v + 1, n)

    def down(v, n):
        return lax.rem(v + n - 1, n)

    sibling = dev(x, y, z, 1 - core)

    barrier = pltpu.get_barrier_semaphore()

    def greet(device):
        pl.semaphore_signal(barrier, inc=1, device_id=device, device_id_type=MESH)

    greet(sibling)
    for xx, yy in ((up(x, 4), y), (down(x, 4), y), (x, up(y, 4)), (x, down(y, 4))):
        greet(dev(xx, yy, z, core))

    own_plane = jnp.where(i == z, 1, 0)
    source = jnp.where(i == 0, 1, 0)

    @pl.when(second)
    def _():
        greet(dev(x, y, up(z, NZ), 1))
        greet(dev(x, y, down(z, NZ), 1))
        for b in range(2):
            for zz in range(NZ):
                is_self = jnp.logical_and(i == z, jnp.logical_and(yl == b, z == zz))

                @pl.when(jnp.logical_not(is_self))
                def _():
                    greet({"rows": b * 2 + 1, "gr": z, "gc": zz})

        pl.semaphore_wait(barrier, 23 - own_plane)

    @pl.when(first)
    def _():
        for d in range(1, NZ):
            greet(dev(x, y, lax.rem(z + d, NZ), 0))
        for b in range(2):

            @pl.when(jnp.logical_not(jnp.logical_and(i == 0, yl == b)))
            def _():
                greet({"rows": b * 2, "gr": 0, "gc": z})

        pl.semaphore_wait(barrier, 12 + 15 * source)

    mine = pl.ds(pl.multiple_of(core * 64, 64), 64)
    theirs = pl.ds(pl.multiple_of((1 - core) * 64, 64), 64)
    chunk[mine, :W] = samp[...]
    chunk[mine, W:] = targ[...]
    swap = pltpu.make_async_remote_copy(
        chunk.at[mine], chunk.at[mine], ex_s, ex_r, device_id=sibling, device_id_type=MESH
    )
    swap.start()
    pltpu.make_async_remote_copy(
        chunk.at[theirs], chunk.at[theirs], ex_s, ex_r, device_id=sibling, device_id_type=MESH
    ).wait_recv()
    own = ai.at[z, yl]
    for b in range(W // N):
        own[b * N : (b + 1) * N, :] = chunk[:, b * N : (b + 1) * N].T
    own[W : W + 8, :] = chunk[:, W:].T[:8]
    lanes = pl.ds(pl.multiple_of(q * N, N), N)

    def plane(buf, c, half_rows):
        sub = half_rows // 2

        def move(h, index, u_off, v_off, off, size, du, dv):
            a, b = (x, y) if h == 0 else (y, x)
            uu, vv = lax.rem(a + u_off + 4, 4), lax.rem(b + v_off + 4, 4)
            tu, tv = lax.rem(a + du + 4, 4), lax.rem(b + dv + 4, 4)
            rows = pl.ds(h * half_rows + off, size)
            item = buf.at[vv, uu, rows] if h == 0 else buf.at[uu, vv, rows]
            to = dev(tu, tv, z, c) if h == 0 else dev(tv, tu, z, c)
            return pltpu.make_async_remote_copy(
                item, item, ag_s.at[h, index], ag_r.at[h, index], device_id=to, device_id_type=MESH
            )

        offsets = (0, -1, 1, 2)

        def u_send(h, n):
            return (
                lambda: move(h, 0, 0, 0, 0, half_rows, 1, 0),
                lambda: move(h, 1, 0, 0, 0, half_rows, -1, 0),
                lambda: move(h, 2, -1, 0, 0, sub, 1, 0),
                lambda: move(h, 3, 1, 0, sub, sub, -1, 0),
            )[n]()

        def u_recv(h, n):
            return (
                lambda: move(h, 0, -1, 0, 0, half_rows, 1, 0),
                lambda: move(h, 1, 1, 0, 0, half_rows, -1, 0),
                lambda: move(h, 2, -2, 0, 0, sub, 1, 0),
                lambda: move(h, 3, 2, 0, sub, sub, -1, 0),
            )[n]()

        def v_send(h, o, n):
            at, u = 4 + 4 * o, offsets[o]
            return (
                lambda: move(h, at, u, 0, 0, half_rows, 0, 1),
                lambda: move(h, at + 1, u, 0, 0, half_rows, 0, -1),
                lambda: move(h, at + 2, u, -1, 0, sub, 0, 1),
                lambda: move(h, at + 3, u, 1, sub, sub, 0, -1),
            )[n]()

        def v_recv(h, o, n):
            at, u = 4 + 4 * o, offsets[o]
            return (
                lambda: move(h, at, u, -1, 0, half_rows, 0, 1),
                lambda: move(h, at + 1, u, 1, 0, half_rows, 0, -1),
                lambda: move(h, at + 2, u, -2, 0, sub, 0, 1),
                lambda: move(h, at + 3, u, 2, sub, sub, 0, -1),
            )[n]()

        def both(step):
            def run():
                for h in range(2):
                    step(h)

            return run

        def begin(h):
            u_send(h, 0).start()
            u_send(h, 1).start()
            v_send(h, 0, 0).start()
            v_send(h, 0, 1).start()

        def u_first(h):
            for n in range(2):
                u_recv(h, n).wait_recv()
                u_send(h, n + 2).start()
                v_send(h, n + 1, 0).start()
                v_send(h, n + 1, 1).start()

        def v_forward(o):
            def step(h):
                for n in range(2):
                    v_recv(h, o, n).wait_recv()
                    v_send(h, o, n + 2).start()

            return step

        def u_second(h):
            u_recv(h, 2).wait_recv()
            u_recv(h, 3).wait_recv()
            v_send(h, 3, 0).start()
            v_send(h, 3, 1).start()

        def end(h):
            for o in range(4):
                v_recv(h, o, 2).wait_recv()
                v_recv(h, o, 3).wait_recv()

        def sent(h):
            for n in range(4):
                u_send(h, n).wait_send()
                for o in range(4):
                    v_send(h, o, n).wait_send()

        return [both(s) for s in (begin, u_first, v_forward(0), u_second, v_forward(1), v_forward(2), v_forward(3), end, sent)]

    def away(n, src, dst):
        return pltpu.make_async_remote_copy(
            src, dst, o_s.at[n], o_r.at[n], device_id=sibling, device_id_type=MESH
        )

    def here(n, src, dst):
        return pltpu.make_async_copy(src, dst, lo.at[n])

    from_second = ((tpre, tpre_o), (gi0, gi0_o), (g0j, g0j_o), (rhs, rhs_o), (top, top_o))
    from_first = ((g00, g00_o), (rg, ridge_o))

    z_over = pltpu.make_async_remote_copy(zb, zb, d_s, d_r, device_id=sibling, device_id_type=MESH)

    @pl.when(first)
    def _():
        def z_piece(b, pp):
            yy, xx = pp // 4, pp % 4
            return pltpu.make_async_remote_copy(
                own.at[pl.ds(pp * 32, 32)],
                zb.at[yy, xx, :, lanes],
                zs_s.at[pp],
                zs_r.at[yl],
                device_id=dev(xx, yy, z, 0),
                device_id_type=MESH,
            )

        def r_piece(pp):
            yy, xx = pp // 4, pp % 4
            return pltpu.make_async_remote_copy(
                rg, rg, rg_s.at[pp], rg_r, device_id=dev(xx, yy, z, 0), device_id_type=MESH
            )

        @pl.when(i == 0)
        def _():
            @pl.when(yl == 0)
            def _():
                rg[...] = ridge[:, :PANEL]

            for pp in range(16):

                @pl.when(p == pp)
                def _():
                    pltpu.make_async_copy(
                        own.at[pl.ds(pp * 32, 32)], zb.at[pp // 4, pp % 4, :, lanes], zs_r.at[yl]
                    ).start()

                @pl.when(p != pp)
                def _():
                    z_piece(0, pp).start()

                    @pl.when(yl == 0)
                    def _():
                        r_piece(pp).start()

        for b in range(2):
            at = zb.at[y, x, :, pl.ds(pl.multiple_of((z * 2 + b) * N, N), N)]
            pltpu.make_async_copy(at, at, zs_r.at[b]).wait()
        pair = zb.at[y, x, :, pl.ds(pl.multiple_of(z * 2 * N, 2 * N), 2 * N)]

        def along(d):
            return pltpu.make_async_remote_copy(
                pair, pair, zz_s.at[d - 1], zz_r.at[d - 1],
                device_id=dev(x, y, lax.rem(z + d, NZ), 0), device_id_type=MESH,
            )

        for d in (1, 7, 2, 6, 3, 5, 4):
            along(d).start()
        for d in (1, 7, 2, 6, 3, 5, 4):
            at = zb.at[y, x, :, pl.ds(pl.multiple_of(lax.rem(z - d + NZ, NZ) * 2 * N, 2 * N), 2 * N)]
            pltpu.make_async_remote_copy(
                at, at, zz_s.at[d - 1], zz_r.at[d - 1], device_id=sibling, device_id_type=MESH
            ).wait_recv()
        steps = plane(zb, 0, 16)
        for step in steps[:-1]:
            step()
        z_over.start()

        for b in range(2):
            rows = slice(b * 8, (b + 1) * 8)
            part = fdot(
                zb[b * 2 : b * 2 + 2].reshape(256, K), zb[...].reshape(PANEL, K), ((1,), (1,))
            )
            g00[b * 256 : (b + 1) * 256, :] = part * (1.0 / K)

        @pl.when(jnp.logical_not(jnp.logical_and(i == 0, yl == 0)))
        def _():
            r_piece(0).wait_recv()

        row = lax.broadcasted_iota(jnp.int32, (PANEL, PANEL), 0)
        col = lax.broadcasted_iota(jnp.int32, (PANEL, PANEL), 1)
        g00[...] = g00[...] + jnp.where(row == col, rg[0:1, :], 0.0)
        for n, (src, dst) in enumerate(from_first):
            away(5 + n, src, dst).start()
            here(5 + n, src, dst).start()

        steps[-1]()
        for d in range(1, NZ):
            along(d).wait_send()

        @pl.when(i == 0)
        def _():
            for pp in range(16):

                @pl.when(p != pp)
                def _():
                    z_piece(0, pp).wait_send()

                    @pl.when(yl == 0)
                    def _():
                        r_piece(pp).wait_send()

        z_over.wait_send()
        for n, (src, dst) in enumerate(from_first):
            away(5 + n, src, dst).wait_send()
            here(5 + n, src, dst).wait()
        for n, (src, dst) in enumerate(from_second):
            away(n, src, dst).wait_recv()

    @pl.when(second)
    def _():
        def ring(way, s, part):
            at = lax.rem(z - s + 1 + NZ, NZ) if way == 0 else lax.rem(z + s - 1, NZ)
            to = dev(x, y, up(z, NZ) if way == 0 else down(z, NZ), 1)
            which = yl if part == 0 else 1 - yl
            item = ai.at[at, which]
            return pltpu.make_async_remote_copy(
                item, item, si_s.at[way, s - 1, part], si_r.at[way, s - 1, part], device_id=to, device_id_type=MESH
            )

        def ring_in(way, s, part):
            at = lax.rem(z - s + NZ, NZ) if way == 0 else lax.rem(z + s, NZ)
            which = yl if part == 0 else 1 - yl
            item = ai.at[at, which]
            return pltpu.make_async_remote_copy(
                item, item, si_s.at[way, s - 1, part], si_r.at[way, s - 1, part], device_id=sibling, device_id_type=MESH
            )

        ring_list = [(s, part, way) for s in (1, 2, 3) for part in range(2) for way in range(2)] + [(4, 0, 0), (4, 1, 1)]

        def s_piece(pp):
            yy, xx = pp // 4, pp % 4
            return pltpu.make_async_remote_copy(
                own.at[pl.ds(pp * 64, 64)],
                sj.at[yy, xx, :, lanes],
                sc_s.at[pp],
                sc_r.at[q],
                device_id=dev(xx, yy, i, 1),
                device_id_type=MESH,
            )

        for pp in range(16):
            is_self = jnp.logical_and(i == z, p == pp)

            @pl.when(is_self)
            def _():
                pltpu.make_async_copy(
                    own.at[pl.ds(pp * 64, 64)], sj.at[pp // 4, pp % 4, :, lanes], sc_r.at[q]
                ).start()

            @pl.when(jnp.logical_not(is_self))
            def _():
                s_piece(pp).start()

        partner = dev(x, yh * 2 + 1 - yl, z, 1)
        trade = pltpu.make_async_remote_copy(own, own, ye_s, ye_r, device_id=partner, device_id_type=MESH)
        trade.start()
        ring(0, 1, 0).start()
        ring(1, 1, 0).start()

        for n in range(16):
            at = sj.at[y, x, :, pl.ds(n * N, N)]
            pltpu.make_async_copy(at, at, sc_r.at[n]).wait()
        steps = plane(sj, 1, 32)

        def advance(s, part, way):
            ring_in(way, s, part).wait_recv()
            if (s + 1, part, way) in ring_list:
                ring(way, s + 1, part).start()

        steps[0]()
        other = ai.at[z, 1 - yl]
        pltpu.make_async_remote_copy(other, other, ye_s, ye_r, device_id=partner, device_id_type=MESH).wait_recv()
        ring(0, 1, 1).start()
        ring(1, 1, 1).start()
        moves = list(ring_list)
        for step in steps[1:-1]:
            for _ in range(2):
                advance(*moves.pop(0))
            step()
        z_over.wait_recv()

        def split_j(n, c):
            for rows in range(2):
                part = pl.ds(pl.multiple_of(n * 64 + rows * 32, 32), 32)
                h, l = high_low(sj[n // 4, lax.rem(n, 4), rows * 32 : rows * 32 + 32, :])
                jh[part, :] = h
                jl[part, :] = l
            part = pl.ds(pl.multiple_of(n * 32, 32), 32)
            h, l = high_low(zb[n // 4, lax.rem(n, 4)])
            zh[part, :] = h
            zl[part, :] = l
            return c

        lax.fori_loop(0, 16, split_j, 0)
        while moves:
            advance(*moves.pop(0))

        def split_i(n, c):
            rows = pl.ds(pl.multiple_of(n * N, N), N)
            for zz in range(NZ):
                for b in range(2):
                    h, l = high_low(ai[zz, b, rows, :])
                    ah[zz, rows, b * N : (b + 1) * N] = h
                    al[zz, rows, b * N : (b + 1) * N] = l
            return c

        lax.fori_loop(0, W // N, split_i, 0)

        tpre[...] = jnp.zeros_like(tpre)
        gi0[...] = jnp.zeros_like(gi0)
        g0j[...] = jnp.zeros_like(g0j)
        rhs[...] = jnp.zeros_like(rhs)
        top[...] = jnp.zeros_like(top)

        def products(zz, c):
            ks = pl.ds(pl.multiple_of(zz * 256, 256), 256)
            across = ((1,), (1,))
            t = jnp.concatenate([ai[zz, 0, W : W + 8, :], ai[zz, 1, W : W + 8, :]], 1)
            th, tl = high_low(t)
            tc = jnp.concatenate([th, tl, th], 1)

            def a_cat(rows, order):
                h, l = ah[zz, rows, :], al[zz, rows, :]
                return jnp.concatenate([h, l, h] if order == 0 else [h, h, l], 1)

            def z_cat(rows, order):
                h, l = zh[rows, ks], zl[rows, ks]
                return jnp.concatenate([h, l, h] if order == 0 else [h, h, l], 1)

            every = pl.ds(0, W)
            half = pl.ds(0, PANEL)

            def columns(n, c):
                rows = pl.ds(pl.multiple_of(n * 256, 256), 256)
                right = jnp.concatenate([jh[rows, ks], jh[rows, ks], jl[rows, ks]], 1)
                tpre[:, rows] += bdot(a_cat(every, 0), right, across)
                g0j[:, rows] += bdot(z_cat(half, 0), right, across)
                rhs[:, rows] += bdot(tc, a_cat(rows, 1), across)
                return c

            lax.fori_loop(0, 4, columns, 0)

            def panel_columns(n, c):
                rows = pl.ds(pl.multiple_of(n * 256, 256), 256)
                right = z_cat(rows, 1)
                gi0[:, rows] += bdot(a_cat(every, 0), right, across)
                top[:, rows] += bdot(tc, right, across)
                return c

            lax.fori_loop(0, 2, panel_columns, 0)
            return c

        lax.fori_loop(0, NZ, products, 0)

        for n, (src, dst) in enumerate(from_second):
            away(n, src, dst).start()
            here(n, src, dst).start()
        steps[-1]()
        for s, part, way in ring_list:
            ring(way, s, part).wait_send()
        trade.wait_send()
        for pp in range(16):
            is_self = jnp.logical_and(i == z, p == pp)

            @pl.when(jnp.logical_not(is_self))
            def _():
                s_piece(pp).wait_send()

        for n, (src, dst) in enumerate(from_second):
            away(n, src, dst).wait_send()
            here(n, src, dst).wait()
        for n, (src, dst) in enumerate(from_first):
            away(5 + n, src, dst).wait_recv()

    swap.wait_send()


def gather(samples, targets, ridge):
    anywhere = pl.BlockSpec(memory_space=pl.ANY)
    inside = pl.BlockSpec(memory_space=pltpu.VMEM)
    dma = pltpu.SemaphoreType.DMA
    shapes = [(W, W), (W, PANEL), (PANEL, W), (PANEL, PANEL), (8, W), (8, PANEL), (8, PANEL)]
    return pl.pallas_call(
        gather_kernel,
        out_shape=[jax.ShapeDtypeStruct(s, f32) for s in shapes],
        in_specs=[inside] * 3,
        out_specs=[anywhere] * len(shapes),
        scratch_shapes=[
            pltpu.VMEM((N, W + N), f32),
            pltpu.VMEM((NZ, 2, W + 8, N), f32),
            pltpu.VMEM((4, 4, 64, K), f32),
            pltpu.VMEM((4, 4, 32, K), f32),
            pltpu.VMEM((8, PANEL), f32),
            pltpu.VMEM((NZ, W, 256), bf16),
            pltpu.VMEM((NZ, W, 256), bf16),
            pltpu.VMEM((W, K), bf16),
            pltpu.VMEM((W, K), bf16),
            pltpu.VMEM((PANEL, K), bf16),
            pltpu.VMEM((PANEL, K), bf16),
            pltpu.VMEM((W, W), f32),
            pltpu.VMEM((W, PANEL), f32),
            pltpu.VMEM((PANEL, W), f32),
            pltpu.VMEM((PANEL, PANEL), f32),
            pltpu.VMEM((8, W), f32),
            pltpu.VMEM((8, PANEL), f32),
            dma, dma, dma, dma,
            dma((2, 4, 2)), dma((2, 4, 2)),
            dma((16,)), dma((16,)),
            dma((16,)), dma((2,)),
            dma((16,)), dma,
            dma((7,)), dma((7,)),
            dma((2, 20)), dma((2, 20)),
            dma, dma,
            dma((7,)), dma((7,)), dma((7,)),
        ],
        compiler_params=pltpu.CompilerParams(
            collective_id=0, has_side_effects=True, vmem_limit_bytes=58 << 20
        ),
        name="gather",
    )(samples, targets, ridge)


def finish_kernel(tpre, gi0, g0j, g00, rhs, top, ridge0, ridge, out, panel, reduced, a, m, ab, mm, pj):
    i, j = lax.axis_index("gr"), lax.axis_index("gc")
    scale = 1.0 / K
    a[...] = g00[...]
    factor_inverse(a, m, ab, mm)
    across, along = ((1,), (1,)), ((1,), (0,))

    def diagonal(shape, value):
        row = lax.broadcasted_iota(jnp.int32, shape, 0)
        col = lax.broadcasted_iota(jnp.int32, shape, 1)
        return jnp.where(row == col, value, 0.0)

    on_i = jnp.where(i == 0, 1.0, 0.0)
    on_j = jnp.where(j == 0, 1.0, 0.0)
    on_ij = jnp.where(i == j, 1.0, 0.0)
    square = (PANEL, PANEL)
    for b in range(2):
        rows = slice(b * PANEL, (b + 1) * PANEL)
        left, right = gi0[rows, :] * scale, g0j[:, rows] * scale
        if b == 0:
            left = left + diagonal(square, ridge0[0:1, :] * on_i)
            right = right + diagonal(square, ridge0[0:1, :] * on_j)
        panel[rows, :] = dot3(left, m[...], across)
        pj[:, rows] = dot3(m[...], right, along)
    for b in range(2):
        cols = slice(b * PANEL, (b + 1) * PANEL)
        for c in range(2):
            rows = slice(c * PANEL, (c + 1) * PANEL)
            tile = tpre[rows, cols] * scale - dot3(panel[rows, :], pj[:, cols], along)
            if b == c:
                tile = tile + diagonal(square, ridge[0:1, cols] * on_ij)
            out[rows, cols] = tile
    solved = fdot(top[...] * scale, m[...], across)
    reduced[...] = rhs[...] * scale - fdot(solved, panel[...], across)


def finish(tpre, gi0, g0j, g00, rhs, top, ridge0, ridge):
    inside = pl.BlockSpec(memory_space=pltpu.VMEM)
    return pl.pallas_call(
        finish_kernel,
        out_shape=[
            jax.ShapeDtypeStruct((W, W), f32),
            jax.ShapeDtypeStruct((W, PANEL), f32),
            jax.ShapeDtypeStruct((8, W), f32),
        ],
        in_specs=[inside] * 8,
        out_specs=[inside] * 3,
        scratch_shapes=[
            pltpu.VMEM((PANEL, PANEL), f32),
            pltpu.VMEM((PANEL, PANEL), f32),
            pltpu.VMEM((N, 2 * N), f32),
            pltpu.VMEM((N, N), f32),
            pltpu.VMEM((PANEL, W), f32),
        ],
        compiler_params=pltpu.CompilerParams(vmem_limit_bytes=50 << 20),
        name="finish",
    )(tpre, gi0, g0j, g00, rhs, top, ridge0, ridge)


def on_device(samples, targets, ridge):
    targets = jnp.broadcast_to(targets[:, None], (targets.shape[0], N))
    ridge = jnp.broadcast_to(ridge[None, :], (8, ridge.shape[0]))
    trailing, panel, reduced = finish(*gather(samples, targets, ridge), ridge)
    return trailing, panel, reduced[0]


def solution(mesh):
    in_specs = (P(("rows", "gc"), "gr"), P(("rows", "gc")), P("gr"))
    out_specs = (P("gr", "gc"), P("gr", None), P("gr"))
    return jax.shard_map(on_device, mesh=mesh, in_specs=in_specs, out_specs=out_specs, check_vma=False)
```

time: 800 us -> 184 us (0.23)
  waiting for transfers between devices: 516 us -> 0 us
  Pallas kernels: 0 us -> 174 us
  other arithmetic: 136 us -> 0 us
  blocking collectives: 51.4 us -> 0 us
  matrix products: 38.3 us -> 0 us
  local copies, waits for them, and re-layouts: 33.7 us -> 9.02 us
  between operations: 18.5 us -> 0.66 us
    psum x4 -> x0, waiting for transfers between devices: 385 us -> none  [broadcast(): return lax.psum(kept, axis)]
    pallas_call x0 -> x2, Pallas kernels: none -> 174 us  [the longest x1 141 us: gather(): pl.pallas_call(gather_kernel, out_shape=[jax.ShapeDtypeStruct(s, f32) for...]
    another operation x17 -> x0, other arithmetic: 121 us -> none  [the longest x14 79.6 us: on_device(): top = jnp.linalg.cholesky(diag_block)]
    all_gather x3 -> x0, waiting for transfers between devices: 79.7 us -> none  [the longest x1 43.1 us: on_device(): lax.all_gather(samples, 'gc', axis=0, tiled=True)]
    reduce_scatter x1 -> x0, waiting for transfers between devices: 50.7 us -> none  [on_device(): lax.psum_scatter(partial_value, 'rows', scatter_dimension=0, tiled=True)]
    unnamed x2 -> x0, blocking collectives: 26.2 us -> none
    another operation x20 -> x0, matrix products: 19.9 us -> none  [the longest x7 9.25 us: on_device(): panel = jax.scipy.linalg.solve_triangular(top, panel_cols.T, lower=True).T]
    psum x1 -> x0, blocking collectives: 19.2 us -> none  [broadcast(): return lax.psum(kept, axis)]
  transfers between devices with their start and end apart: 8 -> 0, of which waited for: 7 -> 0; matrix products, arithmetic and copies ran while one was open for 2% -> 0% of each run, Pallas kernels for 0% -> 0%
where the time goes in v1:
time: 184 us
  Pallas kernels  174 us (95%)
  local copies, waits for them, and re-layouts  9.02 us (5%)
    pallas_call x1, Pallas kernels, gather(): pl.pallas_call(gather_kernel, out_shape=[jax.ShapeDtypeStruct(s, f32) for...  141 us
    pallas_call x1, Pallas kernels, finish(): pl.pallas_call(finish_kernel, out_shape=[jax.ShapeDtypeStruct((W, W), f32...  33 us
    unnamed x12, local copies, waits for them, and re-layouts  5.76 us

profile of v1, /device:TPU:1, one launch (start us, length us, event | category | flops | bytes accessed | tf_op | source)
XLA Modules:
  0.0 183.8 jit_solution(18365884350790099415)
XLA Ops:
  0.6 1.3 broadcast_in_dim.5.ridge
  1.9 1.3 broadcast_in_dim.4.targ
  3.3 141.1 %gather.1 = (f32[1024,1024]{1,0:T(8,128)}, f32[1024,512]{1,0:T(8,128)}, f32[512,1024]{1,0:T(8,128)}, f32[512,512]{1,0:T(8,128)}, f32[8,1024]{1,0:T(8,128)}, /*index=5*/f32[8,512]{1,0:T(8,128)}, f32[8,512]{1,0:T(8,128)}) custom-call(f32[64,1024]{1,0:T(8,128)} %samp.1, f32[64,128]{1,0:T(8,128)} %broadcast_in_dim.4.targ, f32[8,1024]{1,0:T(8,128)} %broadcast_in_dim.5.ridge), custom_call_target="tpu_custom_call" | custom-call | tf_op jit(solution)/shard_map/gather/pallas_call | solution.py:608
  144.4 0.0 copy-start
  144.4 1.6 copy-done
  146.0 0.0 copy-start.1
  146.0 1.2 copy-done.1
  147.2 0.0 copy-start.2
  147.2 0.8 copy-done.2
  148.0 0.0 copy-start.3
  148.0 0.8 copy-done.3
  148.8 0.0 copy-start.4
  148.8 0.7 copy-done.4
  149.5 0.0 copy-start.5
  149.5 0.7 copy-done.5
  150.2 33.0 %finish.1 = (f32[1024,1024]{1,0:T(8,128)}, f32[1024,512]{1,0:T(8,128)}, f32[8,1024]{1,0:T(8,128)S(1)}) custom-call(f32[1024,1024]{1,0:T(8,128)} %get-tuple-element.13.tpre, f32[1024,512]{1,0:T(8,128)S(1)} %copy-done, f32[512,1024]{1,0:T(8,128)} %get-tuple-element.15.g0j, f32[512,512]{1,0:T(8,128)S(1)} %copy-done.1, f32[8,1024]{1,0:T(8,128)S(1)} %copy-done.3, ...), custom_call_target="tpu_custom_call" | custom-call | tf_op jit(solution)/shard_map/finish/pallas_call | solution.py:686
  183.2 0.6 slice.3
Async XLA Ops:
  144.4 1.6 copy-start
  146.0 1.2 copy-start.1
  147.2 0.8 copy-start.2
  148.0 0.8 copy-start.3
  148.8 0.7 copy-start.4
  149.5 0.7 copy-start.5

commit v2 on v1

v2 whole, which is shorter than its diff:
```python
import jax
import jax.numpy as jnp
from jax import lax
from jax.experimental import pallas as pl
from jax.experimental.pallas import tpu as pltpu
from jax.sharding import PartitionSpec as P

f32, bf16 = jnp.float32, jnp.bfloat16
MESH = pl.DeviceIdType.MESH
PANEL = 512
W = 1024
K = 2048
NZ = 8
N = 128
Q = 256
NS = 3


def fdot(a, b, dims=((1,), (0,))):
    return lax.dot_general(a, b, (dims, ((), ())), precision=lax.Precision.HIGHEST, preferred_element_type=f32)


def bdot(a, b, dims=((1,), (0,))):
    return lax.dot_general(a, b, (dims, ((), ())), preferred_element_type=f32)


def high_low(x):
    high = x.astype(bf16)
    return high, (x - high.astype(f32)).astype(bf16)


def split3(x):
    a = x.astype(bf16).astype(f32)
    r = x - a
    b = r.astype(bf16).astype(f32)
    return a, b, r - b


def stack_left(x):
    a, b, c = split3(x)
    return jnp.concatenate([a, a, a, b, b, c], 0).astype(bf16)


def stack_right(x):
    a, b, c = split3(x)
    return jnp.concatenate([a, b, c, a, b, a], 0).astype(bf16)


def dot3(a, b, dims):
    (da,), (db,) = dims
    ah, al = high_low(a)
    bh, bl = high_low(b)
    return bdot(jnp.concatenate([ah, al, ah], da), jnp.concatenate([bh, bh, bl], db), dims)


def row_of(x, i):
    return jnp.broadcast_to(x[i : i + 1, :], (8, x.shape[1]))


def twice(x):
    return jnp.concatenate([x, x], 1)


def strip_factor(s, strip):
    left = strip[:, :N]
    cols = [jnp.take_along_axis(left, jnp.full((8, N), s * 8 + j, jnp.int32), axis=1) for j in range(8)]
    e = {(i, j): row_of(cols[j], i) for j in range(8) for i in range(j, 8)}
    t = [row_of(strip, i) for i in range(8)]
    f, inv, root = {}, [], []
    for k in range(8):
        r = lax.rsqrt(e[k, k])
        r = r * (1.5 - 0.5 * e[k, k] * r * r)
        p = r * r
        p = p * (2.0 - e[k, k] * p)
        inv.append(p)
        root.append(r)
        for i in range(k + 1, 8):
            f[i, k] = e[i, k] * p
        for j in range(k + 1, 8):
            for i in range(j, 8):
                e[i, j] = e[i, j] - f[i, k] * e[j, k]
        for i in range(k + 1, 8):
            t[i] = t[i] - twice(f[i, k]) * t[k]
    y = [None] * 8
    for i in reversed(range(8)):
        acc = t[i] * twice(inv[i])
        for k in range(i + 1, 8):
            acc = acc - twice(f[k, i]) * y[k]
        y[i] = acc
    row = lax.broadcasted_iota(jnp.int32, (8, N), 0)

    def assemble(parts):
        out = parts[0]
        rows = row if out.shape[1] == N else twice(row)
        for i in range(1, 8):
            out = jnp.where(rows == i, parts[i], out)
        return out

    return assemble(y), assemble([t[i][:, N:] * root[i] for i in range(8)]), y


def factor_block(ab, m_ref):
    def body(s, carry):
        strip, left, right = carry
        ab[...] = ab[...] - bdot(left, right)
        whole, inverse_rows, y = strip_factor(s, strip)
        m_ref[pl.ds(pl.multiple_of(s * 8, 8), 8), :] = inverse_rows
        after = lax.rem(s + 1, 16)
        rows = ab[pl.ds(pl.multiple_of(after * 8, 8), 8), :]
        terms = []
        for j in range(8):
            c = jnp.take_along_axis(rows[:, :N], jnp.full((8, N), s * 8 + j, jnp.int32), axis=1)
            terms.append(twice(c) * y[j])
        while len(terms) > 1:
            terms = [terms[i] + terms[i + 1] for i in range(0, len(terms), 2)]
        return rows - terms[0], stack_left(strip[:, :N]).T, stack_right(whole)

    lax.fori_loop(0, 16, body, (ab[0:8, :], jnp.zeros((N, 48), bf16), jnp.zeros((48, 2 * N), bf16)))


def factor_inverse(a, b, ab, m):
    b[...] = jnp.zeros_like(b)
    eye = jnp.where(
        lax.broadcasted_iota(jnp.int32, (N, N), 0) == lax.broadcasted_iota(jnp.int32, (N, N), 1), 1.0, 0.0
    )
    blocks = PANEL // N
    for k in range(blocks):
        now, rest = slice(k * N, (k + 1) * N), slice((k + 1) * N, PANEL)
        ab[:, :N] = a[now, now]
        ab[:, N:] = eye
        factor_block(ab, m)
        b[now, now] = m[...]
        if k:
            b[now, : k * N] = fdot(m[...], b[now, : k * N])
        if k < blocks - 1:
            u = fdot(m[...], a[now, rest])
            a[rest, rest] = a[rest, rest] - fdot(u, u, ((0,), (0,)))
            b[rest, : (k + 1) * N] = b[rest, : (k + 1) * N] - fdot(u, b[now, : (k + 1) * N], ((0,), (0,)))


def kernel(
    samp, targ, ridge,
    out_o, panel_o, red_o,
    chunk, ai, sj, zb, stage, rg, azh, azl, tg, gi0, acc, g00, inverse, ab, mm, panel, rhs, top, red,
    ex_s, ex_r, ye_s, ye_r, si_s, si_r, sc_s, sc_r, zs_s, zs_r, rg_s, rg_r, zz_s, zz_r, ag_s, ag_r, h_s, h_r, lo,
):
    r, i, z = lax.axis_index("rows"), lax.axis_index("gr"), lax.axis_index("gc")
    core, yl = lax.rem(r, 2), r // 2
    x, yh = i // 2, lax.rem(i, 2)
    y = yh * 2 + yl
    p = y * 4 + x
    first, second = core == 0, core == 1
    scale = 1.0 / K
    across, along = ((1,), (1,)), ((1,), (0,))

    def dev(xx, yy, zz, c):
        return {"rows": lax.rem(yy, 2) * 2 + c, "gr": xx * 2 + yy // 2, "gc": zz}

    def up(v, n):
        return lax.rem(v + 1, n)

    def down(v, n):
        return lax.rem(v + n - 1, n)

    sibling = dev(x, y, z, 1 - core)

    barrier = pltpu.get_barrier_semaphore()

    def greet(device):
        pl.semaphore_signal(barrier, inc=1, device_id=device, device_id_type=MESH)

    greet(sibling)
    for d in range(1, NZ):
        greet(dev(x, y, lax.rem(z + d, NZ), core))
    source = jnp.where(i == 0, 1, 0)

    @pl.when(second)
    def _():
        for d in range(1, 16):
            pp = lax.rem(p + d, 16)
            greet(dev(lax.rem(pp, 4), pp // 4, z, 1))
        pl.semaphore_wait(barrier, 23)

    @pl.when(first)
    def _():
        for xx, yy in ((up(x, 4), y), (down(x, 4), y), (x, up(y, 4)), (x, down(y, 4))):
            greet(dev(xx, yy, z, 0))
        for b in range(2):

            @pl.when(jnp.logical_not(jnp.logical_and(i == 0, yl == b)))
            def _():
                greet({"rows": b * 2, "gr": 0, "gc": z})

        pl.semaphore_wait(barrier, 12 + 15 * source)

    mine = pl.ds(pl.multiple_of(core * 64, 64), 64)
    theirs = pl.ds(pl.multiple_of((1 - core) * 64, 64), 64)
    chunk[mine, :W] = samp[...]
    chunk[mine, W:] = targ[...]
    swap = pltpu.make_async_remote_copy(
        chunk.at[mine], chunk.at[mine], ex_s, ex_r, device_id=sibling, device_id_type=MESH
    )
    swap.start()
    pltpu.make_async_remote_copy(
        chunk.at[theirs], chunk.at[theirs], ex_s, ex_r, device_id=sibling, device_id_type=MESH
    ).wait_recv()
    own = ai.at[z, yl]
    for b in range(W // N):
        own[b * N : (b + 1) * N, :] = chunk[:, b * N : (b + 1) * N].T
    own[W : W + 8, :] = chunk[:, W:].T[:8]

    def pair_lanes(zz):
        return pl.ds(pl.multiple_of(zz * 2 * N, 2 * N), 2 * N)

    def lanes(zz, b):
        return pl.ds(pl.multiple_of((zz * 2 + b) * N, N), N)

    def plane(buf, c, half_rows):
        sub = half_rows // 2

        def move(h, index, u_off, v_off, off, size, du, dv):
            a, b = (x, y) if h == 0 else (y, x)
            uu, vv = lax.rem(a + u_off + 4, 4), lax.rem(b + v_off + 4, 4)
            tu, tv = lax.rem(a + du + 4, 4), lax.rem(b + dv + 4, 4)
            rows = pl.ds(h * half_rows + off, size)
            item = buf.at[vv, uu, rows] if h == 0 else buf.at[uu, vv, rows]
            to = dev(tu, tv, z, c) if h == 0 else dev(tv, tu, z, c)
            return pltpu.make_async_remote_copy(
                item, item, ag_s.at[h, index], ag_r.at[h, index], device_id=to, device_id_type=MESH
            )

        offsets = (0, -1, 1, 2)

        def u_send(h, n):
            return (
                lambda: move(h, 0, 0, 0, 0, half_rows, 1, 0),
                lambda: move(h, 1, 0, 0, 0, half_rows, -1, 0),
                lambda: move(h, 2, -1, 0, 0, sub, 1, 0),
                lambda: move(h, 3, 1, 0, sub, sub, -1, 0),
            )[n]()

        def u_recv(h, n):
            return (
                lambda: move(h, 0, -1, 0, 0, half_rows, 1, 0),
                lambda: move(h, 1, 1, 0, 0, half_rows, -1, 0),
                lambda: move(h, 2, -2, 0, 0, sub, 1, 0),
                lambda: move(h, 3, 2, 0, sub, sub, -1, 0),
            )[n]()

        def v_send(h, o, n):
            at, u = 4 + 4 * o, offsets[o]
            return (
                lambda: move(h, at, u, 0, 0, half_rows, 0, 1),
                lambda: move(h, at + 1, u, 0, 0, half_rows, 0, -1),
                lambda: move(h, at + 2, u, -1, 0, sub, 0, 1),
                lambda: move(h, at + 3, u, 1, sub, sub, 0, -1),
            )[n]()

        def v_recv(h, o, n):
            at, u = 4 + 4 * o, offsets[o]
            return (
                lambda: move(h, at, u, -1, 0, half_rows, 0, 1),
                lambda: move(h, at + 1, u, 1, 0, half_rows, 0, -1),
                lambda: move(h, at + 2, u, -2, 0, sub, 0, 1),
                lambda: move(h, at + 3, u, 2, sub, sub, 0, -1),
            )[n]()

        def both(step):
            def run():
                for h in range(2):
                    step(h)

            return run

        def begin(h):
            u_send(h, 0).start()
            u_send(h, 1).start()
            v_send(h, 0, 0).start()
            v_send(h, 0, 1).start()

        def u_first(h):
            for n in range(2):
                u_recv(h, n).wait_recv()
                u_send(h, n + 2).start()
                v_send(h, n + 1, 0).start()
                v_send(h, n + 1, 1).start()

        def v_forward(o):
            def step(h):
                for n in range(2):
                    v_recv(h, o, n).wait_recv()
                    v_send(h, o, n + 2).start()

            return step

        def u_second(h):
            u_recv(h, 2).wait_recv()
            u_recv(h, 3).wait_recv()
            v_send(h, 3, 0).start()
            v_send(h, 3, 1).start()

        def end(h):
            for o in range(4):
                v_recv(h, o, 2).wait_recv()
                v_recv(h, o, 3).wait_recv()

        def sent(h):
            for n in range(4):
                u_send(h, n).wait_send()
                for o in range(4):
                    v_send(h, o, n).wait_send()

        return [both(s) for s in (begin, u_first, v_forward(0), u_second, v_forward(1), v_forward(2), v_forward(3), end, sent)]

    def give(n, src, dst):
        return pltpu.make_async_remote_copy(
            src, dst, h_s.at[n], h_r.at[n], device_id=sibling, device_id_type=MESH
        )

    def part(n):
        return pl.ds(pl.multiple_of(n * Q, Q), Q)

    give_gi0 = give(0, gi0, gi0)
    give_rhs = give(1, rhs, rhs)
    give_top = give(2, top, top)
    give_z = give(7, zb, zb)
    give_inverse = give(8, inverse, inverse)
    give_panel = give(9, panel, panel)
    give_red = give(10, red, red_o)
    keep_panel = pltpu.make_async_copy(panel, panel_o, lo.at[4])
    keep_red = pltpu.make_async_copy(red, red_o, lo.at[5])

    def give_tile(n):
        return give(3 + n, tg.at[:, part(n)], tg.at[:, part(n)])

    def give_out(n):
        return give(11 + n, tg.at[pl.ds(0, W), part(n)], out_o.at[:, part(n)])

    def keep_out(n):
        return pltpu.make_async_copy(tg.at[pl.ds(0, W), part(n)], out_o.at[:, part(n)], lo.at[n])

    def diagonal(shape, shift, value):
        row = lax.broadcasted_iota(jnp.int32, shape, 0)
        col = lax.broadcasted_iota(jnp.int32, shape, 1)
        return jnp.where(row == col + shift, value, 0.0)

    on_i = jnp.where(i == 0, 1.0, 0.0)
    on_j = jnp.where(z == 0, 1.0, 0.0)
    on_ij = jnp.where(i == z, 1.0, 0.0)

    def update(n):
        right = tg[W:, part(n)] * scale
        if n < 2:
            right = right + diagonal((PANEL, Q), n * Q, rg[0:1, n * Q : (n + 1) * Q] * on_j)
        column_factor = dot3(inverse[...], right, along)
        tile = tg[:W, part(n)] * scale - dot3(panel[...], column_factor, along)
        tg[:W, part(n)] = tile + diagonal((W, Q), n * Q, ridge[0:1, n * Q : (n + 1) * Q] * on_ij)
        keep_out(n).start()
        give_out(n).start()

    @pl.when(first)
    def _():
        def z_piece(d):
            pp = lax.rem(p + d, 16)
            return pltpu.make_async_remote_copy(
                own.at[pl.ds(pl.multiple_of(pp * 32, 32), 32)],
                zb.at[pp // 4, lax.rem(pp, 4), :, lanes(z, yl)],
                zs_s.at[d], zs_r.at[yl],
                device_id=dev(lax.rem(pp, 4), pp // 4, z, 0), device_id_type=MESH,
            )

        def r_piece(d):
            pp = lax.rem(p + d, 16)
            return pltpu.make_async_remote_copy(
                rg, rg, rg_s.at[d], rg_r, device_id=dev(lax.rem(pp, 4), pp // 4, z, 0), device_id_type=MESH
            )

        @pl.when(i == 0)
        def _():
            pltpu.make_async_copy(
                own.at[pl.ds(pl.multiple_of(p * 32, 32), 32)], zb.at[y, x, :, lanes(z, yl)], zs_r.at[yl]
            ).start()
            for d in range(1, 16):
                z_piece(d).start()

            @pl.when(yl == 0)
            def _():
                rg[...] = ridge[:, :PANEL]
                for d in range(1, 16):
                    r_piece(d).start()

        for b in range(2):
            at = zb.at[y, x, :, lanes(z, b)]
            pltpu.make_async_copy(at, at, zs_r.at[b]).wait()

        def z_plane(d):
            item = zb.at[y, x, :, pair_lanes(z)]
            return pltpu.make_async_remote_copy(
                item, item, zz_s.at[d - 1], zz_r.at[d - 1],
                device_id=dev(x, y, lax.rem(z + d, NZ), 0), device_id_type=MESH,
            )

        for d in (1, 7, 2, 6, 3, 5, 4):
            z_plane(d).start()
        for d in (1, 7, 2, 6, 3, 5, 4):
            item = zb.at[y, x, :, pair_lanes(lax.rem(z - d + NZ, NZ))]
            pltpu.make_async_remote_copy(
                item, item, zz_s.at[d - 1], zz_r.at[d - 1], device_id=sibling, device_id_type=MESH
            ).wait_recv()
        steps = plane(zb, 0, 16)
        for step in steps[:-1]:
            step()
        give_z.start()

        for b in range(2):
            rows = zb[b * 2 : b * 2 + 2].reshape(256, K)
            g00[b * 256 : (b + 1) * 256, :] = fdot(rows, zb[...].reshape(PANEL, K), across) * scale

        @pl.when(jnp.logical_not(jnp.logical_and(i == 0, yl == 0)))
        def _():
            r_piece(1).wait_recv()

        g00[...] = g00[...] + diagonal((PANEL, PANEL), 0, rg[0:1, :])
        factor_inverse(g00, inverse, ab, mm)
        give_inverse.start()

        give_gi0.wait_recv()
        for b in range(2):
            rows = slice(b * PANEL, (b + 1) * PANEL)
            panel[rows, :] = dot3(gi0[rows, :], inverse[...], across)
        give_panel.start()
        keep_panel.start()
        for n in range(NS):
            give_tile(n).wait_recv()
            update(n)
        give_rhs.wait_recv()
        give_top.wait_recv()
        solved = fdot(top[...], inverse[...], across)
        red[...] = rhs[...] - fdot(solved, panel[...], across)
        give_red.start()
        keep_red.start()

        steps[-1]()
        for d in range(1, NZ):
            z_plane(d).wait_send()

        @pl.when(i == 0)
        def _():
            for d in range(1, 16):
                z_piece(d).wait_send()

            @pl.when(yl == 0)
            def _():
                for d in range(1, 16):
                    r_piece(d).wait_send()

        give_z.wait_send()
        give_inverse.wait_send()
        give_panel.wait_send()
        give_red.wait_send()
        keep_panel.wait()
        keep_red.wait()
        for n in range(NS):
            keep_out(n).wait()
            give_out(n).wait_send()
        for n in range(NS, 4):
            give_out(n).wait_recv()

    @pl.when(second)
    def _():
        def ring(way, s, b):
            at = lax.rem(z - s + 1 + NZ, NZ) if way == 0 else lax.rem(z + s - 1, NZ)
            item = ai.at[at, yl if b == 0 else 1 - yl]
            to = dev(x, y, up(z, NZ) if way == 0 else down(z, NZ), 1)
            return pltpu.make_async_remote_copy(
                item, item, si_s.at[way, s - 1, b], si_r.at[way, s - 1, b], device_id=to, device_id_type=MESH
            )

        def ring_in(way, s, b):
            at = lax.rem(z - s + NZ, NZ) if way == 0 else lax.rem(z + s, NZ)
            item = ai.at[at, yl if b == 0 else 1 - yl]
            return pltpu.make_async_remote_copy(
                item, item, si_s.at[way, s - 1, b], si_r.at[way, s - 1, b], device_id=sibling, device_id_type=MESH
            )

        ring_list = [(s, b, way) for s in (1, 2, 3) for b in range(2) for way in range(2)] + [(4, 0, 0), (4, 1, 1)]

        def s_piece(d):
            pp = lax.rem(p + d, 16)
            return pltpu.make_async_remote_copy(
                own.at[pl.ds(pl.multiple_of(pp * 64, 64), 64)],
                stage.at[i, :, pl.ds(pl.multiple_of(yl * N, N), N)],
                sc_s.at[d], sc_r.at[i * 2 + yl],
                device_id=dev(lax.rem(pp, 4), pp // 4, z, 1), device_id_type=MESH,
            )

        for d in range(1, 16):
            s_piece(d).start()
        pltpu.make_async_copy(
            own.at[pl.ds(pl.multiple_of(p * 64, 64), 64)],
            stage.at[i, :, pl.ds(pl.multiple_of(yl * N, N), N)],
            sc_r.at[i * 2 + yl],
        ).start()
        partner = dev(x, yh * 2 + 1 - yl, z, 1)
        trade = pltpu.make_async_remote_copy(own, own, ye_s, ye_r, device_id=partner, device_id_type=MESH)
        trade.start()
        ring(0, 1, 0).start()
        ring(1, 1, 0).start()
        for n in range(16):
            at = stage.at[n // 2, :, pl.ds((n % 2) * N, N)]
            pltpu.make_async_copy(at, at, sc_r.at[n]).wait()

        def s_plane(d):
            to = lax.rem(z + d, NZ)
            return pltpu.make_async_remote_copy(
                stage.at[to], sj.at[y, x, :, pair_lanes(z)], zz_s.at[d - 1], zz_r.at[d - 1],
                device_id=dev(x, y, to, 1), device_id_type=MESH,
            )

        for d in (1, 7, 2, 6, 3, 5, 4):
            s_plane(d).start()
        stay = pltpu.make_async_copy(stage.at[z], sj.at[y, x, :, pair_lanes(z)], lo.at[6])
        stay.start()
        other = ai.at[z, 1 - yl]
        pltpu.make_async_remote_copy(other, other, ye_s, ye_r, device_id=partner, device_id_type=MESH).wait_recv()
        ring(0, 1, 1).start()
        ring(1, 1, 1).start()
        for d in (1, 7, 2, 6, 3, 5, 4):
            item = sj.at[y, x, :, pair_lanes(lax.rem(z - d + NZ, NZ))]
            pltpu.make_async_remote_copy(
                item, item, zz_s.at[d - 1], zz_r.at[d - 1], device_id=sibling, device_id_type=MESH
            ).wait_recv()
        stay.wait()
        steps = plane(sj, 1, 32)

        def advance(s, b, way):
            ring_in(way, s, b).wait_recv()
            if (s + 1, b, way) in ring_list:
                ring(way, s + 1, b).start()

        moves = list(ring_list)
        steps[0]()
        for step in steps[1:-1]:
            if len(moves) > 2:
                advance(*moves.pop(0))
                advance(*moves.pop(0))
            step()
        give_z.wait_recv()

        def group(offsets, fresh):
            items = [lax.rem(z + o + NZ, NZ) for o in offsets]

            def put(ref, index, value):
                if fresh:
                    ref[index] = value
                else:
                    ref[index] += value

            def target(it, b):
                return ai[it, b, W : W + 1, :]

            def split_rows(n, c):
                rows = pl.ds(pl.multiple_of(n * N, N), N)
                total = jnp.zeros((N, N), f32)
                for slot, it in enumerate(items):
                    for b in range(2):
                        v = ai[it, b, rows, :]
                        h, l = high_low(v)
                        azh[slot, rows, b * N : (b + 1) * N] = h
                        azl[slot, rows, b * N : (b + 1) * N] = l
                        total = total + v * target(it, b)
                put(acc, (rows, slice(None)), total)
                return c

            lax.fori_loop(0, W // N, split_rows, 0)

            def split_leading(n, c):
                rows = pl.ds(pl.multiple_of(W + n * N, N), N)
                total = jnp.zeros((N, N), f32)
                for slot, it in enumerate(items):
                    v = zb[n, :, :, pair_lanes(it)].reshape(N, 2 * N)
                    h, l = high_low(v)
                    azh[slot, rows, :] = h
                    azl[slot, rows, :] = l
                    for b in range(2):
                        total = total + v[:, b * N : (b + 1) * N] * target(it, b)
                put(acc, (rows, slice(None)), total)
                return c

            lax.fori_loop(0, PANEL // N, split_leading, 0)

            def left(rows):
                parts = []
                for slot in range(4):
                    h, l = azh[slot, rows, :], azl[slot, rows, :]
                    parts += [h, l, h]
                return jnp.concatenate(parts, 1)

            def panel_columns(n, c):
                rows = pl.ds(pl.multiple_of(W + n * Q, Q), Q)
                parts = []
                for slot in range(4):
                    h, l = azh[slot, rows, :], azl[slot, rows, :]
                    parts += [h, h, l]
                put(gi0, (slice(None), part(n)), bdot(left(pl.ds(0, W)), jnp.concatenate(parts, 1), across))
                return c

            lax.fori_loop(0, PANEL // Q, panel_columns, 0)
            if not fresh:
                gi0[...] = gi0[...] * scale
                gi0[:PANEL, :] += diagonal((PANEL, PANEL), 0, ridge[0:1, :PANEL] * on_i)
                give_gi0.start()

            def columns(n, c):
                parts = []
                for it in items:
                    h, l = high_low(sj[n, :, :, pair_lanes(it)].reshape(Q, 2 * N))
                    parts += [h, h, l]
                put(tg, (slice(None), part(n)), bdot(left(pl.ds(0, W + PANEL)), jnp.concatenate(parts, 1), across))
                if not fresh:

                    @pl.when(n < NS)
                    def _():
                        give_tile(n).start()

                return c

            lax.fori_loop(0, 4, columns, 0)

        group((0, -1, 1, -2), True)
        while moves:
            advance(*moves.pop(0))
        group((2, -3, 3, 4), False)
        ones = jnp.full((8, N), scale, f32)
        rhs[...] = fdot(ones, acc[:W, :], across)
        top[...] = fdot(ones, acc[W:, :], across)
        give_rhs.start()
        give_top.start()
        give_inverse.wait_recv()
        give_panel.wait_recv()
        keep_panel.start()
        for n in range(NS, 4):
            update(n)

        steps[-1]()
        for s, b, way in ring_list:
            ring(way, s, b).wait_send()
        trade.wait_send()
        for d in range(1, 16):
            s_piece(d).wait_send()
        for d in range(1, NZ):
            s_plane(d).wait_send()
        give_gi0.wait_send()
        give_rhs.wait_send()
        give_top.wait_send()
        keep_panel.wait()
        for n in range(NS):
            give_tile(n).wait_send()
            give_out(n).wait_recv()
        for n in range(NS, 4):
            keep_out(n).wait()
            give_out(n).wait_send()
        give_red.wait_recv()

    swap.wait_send()


def on_device(samples, targets, ridge):
    targets = jnp.broadcast_to(targets[:, None], (targets.shape[0], N))
    ridge = jnp.broadcast_to(ridge[None, :], (8, ridge.shape[0]))
    anywhere = pl.BlockSpec(memory_space=pl.ANY)
    inside = pl.BlockSpec(memory_space=pltpu.VMEM)
    dma = pltpu.SemaphoreType.DMA
    shapes = [(W, W), (W, PANEL), (8, W)]
    trailing, panel, reduced = pl.pallas_call(
        kernel,
        out_shape=[jax.ShapeDtypeStruct(s, f32) for s in shapes],
        in_specs=[inside] * 3,
        out_specs=[anywhere] * len(shapes),
        scratch_shapes=[
            pltpu.VMEM((N, W + N), f32),
            pltpu.VMEM((NZ, 2, W + 8, N), f32),
            pltpu.VMEM((4, 4, 64, K), f32),
            pltpu.VMEM((4, 4, 32, K), f32),
            pltpu.VMEM((NZ, 64, 2 * N), f32),
            pltpu.VMEM((8, PANEL), f32),
            pltpu.VMEM((4, W + PANEL, 2 * N), bf16),
            pltpu.VMEM((4, W + PANEL, 2 * N), bf16),
            pltpu.VMEM((W + PANEL, W), f32),
            pltpu.VMEM((W, PANEL), f32),
            pltpu.VMEM((W + PANEL, N), f32),
            pltpu.VMEM((PANEL, PANEL), f32),
            pltpu.VMEM((PANEL, PANEL), f32),
            pltpu.VMEM((N, 2 * N), f32),
            pltpu.VMEM((N, N), f32),
            pltpu.VMEM((W, PANEL), f32),
            pltpu.VMEM((8, W), f32),
            pltpu.VMEM((8, PANEL), f32),
            pltpu.VMEM((8, W), f32),
            dma, dma, dma, dma,
            dma((2, 4, 2)), dma((2, 4, 2)),
            dma((16,)), dma((16,)),
            dma((16,)), dma((2,)),
            dma((16,)), dma,
            dma((7,)), dma((7,)),
            dma((2, 20)), dma((2, 20)),
            dma((15,)), dma((15,)), dma((7,)),
        ],
        compiler_params=pltpu.CompilerParams(
            collective_id=0, has_side_effects=True, vmem_limit_bytes=56 << 20
        ),
        name="ridge_panel",
    )(samples, targets, ridge)
    return trailing, panel, reduced[0]


def solution(mesh):
    in_specs = (P(("rows", "gc"), "gr"), P(("rows", "gc")), P("gr"))
    out_specs = (P("gr", "gc"), P("gr", None), P("gr"))
    return jax.shard_map(on_device, mesh=mesh, in_specs=in_specs, out_specs=out_specs, check_vma=False)
```

time: 184 us -> 121 us (0.66)
  Pallas kernels: 174 us -> 110 us
    pallas_call x2 -> x1, Pallas kernels: 174 us -> 110 us  [on_device(): pl.pallas_call(kernel, out_shape=[jax.ShapeDtypeStruct(s, f32) for s in s...]
    unnamed x12 -> x4, local copies, waits for them, and re-layouts: 5.76 us -> 6.26 us
where the time goes in v2:
time: 121 us; the launch traced here: 120 us
  Pallas kernels  110 us (91%)
  local copies, waits for them, and re-layouts  10.3 us (9%)
    pallas_call x1, Pallas kernels, on_device(): pl.pallas_call(kernel, out_shape=[jax.ShapeDtypeStruct(s, f32) for s in s...  110 us
    unnamed x4, local copies, waits for them, and re-layouts  6.26 us

profile of v2, /device:TPU:1, one launch (start us, length us, event | category | flops | bytes accessed | tf_op | source)
XLA Modules:
  0.0 120.4 jit_solution(14383714121186847126)
XLA Ops:
  0.6 1.3 %broadcast_in_dim.4.targ = f32[64,128]{1,0:T(8,128)} broadcast(f32[64]{0:T(128)} %param.4), dimensions={0} | broadcast | bytes 33024 | tf_op jit(solution)/shard_map/broadcast_in_dim | solution.py:669
  2.0 1.3 %broadcast_in_dim.5.ridge = f32[8,1024]{1,0:T(8,128)} broadcast(f32[1024]{0:T(1024)} %param.5), dimensions={1} | broadcast | bytes 36864 | tf_op jit(solution)/shard_map/broadcast_in_dim | solution.py:670
  3.3 109.5 %ridge_panel.1 = (f32[1024,1024]{1,0:T(8,128)}, f32[1024,512]{1,0:T(8,128)}, f32[8,1024]{1,0:T(8,128)}) custom-call(f32[64,1024]{1,0:T(8,128)} %samp.1, f32[64,128]{1,0:T(8,128)} %broadcast_in_dim.4.targ, f32[8,1024]{1,0:T(8,128)} %broadcast_in_dim.5.ridge), custom_call_target="tpu_custom_call" | custom-call | tf_op jit(solution)/shard_map/ridge_panel/pallas_call | solution.py:675
  112.8 1.4 %slice.3 = f32[1,1024]{1,0:T(1,128)} slice(f32[8,1024]{1,0:T(8,128)} %get-tuple-element.8), slice={[0:1], [0:1024]} | slice | bytes 8192 | tf_op jit(solution)/shard_map/slice | solution.py:714
  114.2 0.0 copy-start
  114.2 4.9 %copy.8 = f32[1024,1024]{1,0:T(8,128)} copy(f32[1024,1024]{1,0:T(8,128)} %get-tuple-element.12) | data formatting | bytes 8388608
  119.1 0.0 copy-done
  119.1 1.3 %copy.9 = f32[1024,512]{1,0:T(8,128)} copy(f32[1024,512]{1,0:T(8,128)S(1)} %copy-done) | data formatting | bytes 4194304
Async XLA Ops:
  114.2 4.9 %copy-start = (f32[1024,512]{1,0:T(8,128)S(1)}, f32[1024,512]{1,0:T(8,128)}, u32[]{:S(2)}) copy-start(f32[1024,512]{1,0:T(8,128)} %get-tuple-element.13) | copy-start | bytes 6291460

commit v3 on v2

--- a/solution.py
+++ b/solution.py
@@ -13,7 +13,7 @@
 NZ = 8
 N = 128
 Q = 256
-NS = 3
+NS = 2
 
 
 def fdot(a, b, dims=((1,), (0,))):
@@ -141,7 +141,7 @@
 def kernel(
     samp, targ, ridge,
     out_o, panel_o, red_o,
-    chunk, ai, sj, zb, stage, rg, azh, azl, tg, gi0, acc, g00, inverse, ab, mm, panel, rhs, top, red,
+    chunk, tr, ai, sj, zb, stage, rg, azh, azl, tg, gi0, acc, g00, inverse, ab, mm, panel, rhs, top, red,
     ex_s, ex_r, ye_s, ye_r, si_s, si_r, sc_s, sc_r, zs_s, zs_r, rg_s, rg_r, zz_s, zz_r, ag_s, ag_r, h_s, h_r, lo,
 ):
     r, i, z = lax.axis_index("rows"), lax.axis_index("gr"), lax.axis_index("gc")
@@ -195,19 +195,27 @@
 
     mine = pl.ds(pl.multiple_of(core * 64, 64), 64)
     theirs = pl.ds(pl.multiple_of((1 - core) * 64, 64), 64)
-    chunk[mine, :W] = samp[...]
-    chunk[mine, W:] = targ[...]
+    chunk[mine, :] = samp[...]
+    tr[core, :, :64] = jnp.broadcast_to(targ[...], (8, 64))
     swap = pltpu.make_async_remote_copy(
-        chunk.at[mine], chunk.at[mine], ex_s, ex_r, device_id=sibling, device_id_type=MESH
+        chunk.at[mine], chunk.at[mine], ex_s.at[0], ex_r.at[0], device_id=sibling, device_id_type=MESH
     )
     swap.start()
+    swap_targets = pltpu.make_async_remote_copy(
+        tr.at[core], tr.at[core], ex_s.at[1], ex_r.at[1], device_id=sibling, device_id_type=MESH
+    )
+    swap_targets.start()
     pltpu.make_async_remote_copy(
-        chunk.at[theirs], chunk.at[theirs], ex_s, ex_r, device_id=sibling, device_id_type=MESH
+        chunk.at[theirs], chunk.at[theirs], ex_s.at[0], ex_r.at[0], device_id=sibling, device_id_type=MESH
     ).wait_recv()
     own = ai.at[z, yl]
     for b in range(W // N):
         own[b * N : (b + 1) * N, :] = chunk[:, b * N : (b + 1) * N].T
-    own[W : W + 8, :] = chunk[:, W:].T[:8]
+    pltpu.make_async_remote_copy(
+        tr.at[1 - core], tr.at[1 - core], ex_s.at[1], ex_r.at[1], device_id=sibling, device_id_type=MESH
+    ).wait_recv()
+    lane = lax.broadcasted_iota(jnp.int32, (8, N), 1)
+    own[W : W + 8, :] = jnp.where(lane < 64, tr[0], pltpu.roll(tr[1], 64, 1))
 
     def pair_lanes(zz):
         return pl.ds(pl.multiple_of(zz * 2 * N, 2 * N), 2 * N)
@@ -215,8 +223,14 @@
     def lanes(zz, b):
         return pl.ds(pl.multiple_of((zz * 2 + b) * N, N), N)
 
-    def plane(buf, c, half_rows):
+    def plane(buf, c, half_rows, pass_on=None):
         sub = half_rows // 2
+
+        def arrived(copy):
+            copy.wait_recv()
+            if pass_on is not None:
+                pass_on(copy.src_ref)
+
 
         def move(h, index, u_off, v_off, off, size, du, dv):
             a, b = (x, y) if h == 0 else (y, x)
@@ -273,14 +287,17 @@
             return run
 
         def begin(h):
-            u_send(h, 0).start()
+            first_copy = u_send(h, 0)
+            first_copy.start()
+            if pass_on is not None:
+                pass_on(first_copy.src_ref)
             u_send(h, 1).start()
             v_send(h, 0, 0).start()
             v_send(h, 0, 1).start()
 
         def u_first(h):
             for n in range(2):
-                u_recv(h, n).wait_recv()
+                arrived(u_recv(h, n))
                 u_send(h, n + 2).start()
                 v_send(h, n + 1, 0).start()
                 v_send(h, n + 1, 1).start()
@@ -288,21 +305,21 @@
         def v_forward(o):
             def step(h):
                 for n in range(2):
-                    v_recv(h, o, n).wait_recv()
+                    arrived(v_recv(h, o, n))
                     v_send(h, o, n + 2).start()
 
             return step
 
         def u_second(h):
-            u_recv(h, 2).wait_recv()
-            u_recv(h, 3).wait_recv()
+            arrived(u_recv(h, 2))
+            arrived(u_recv(h, 3))
             v_send(h, 3, 0).start()
             v_send(h, 3, 1).start()
 
         def end(h):
             for o in range(4):
-                v_recv(h, o, 2).wait_recv()
-                v_recv(h, o, 3).wait_recv()
+                arrived(v_recv(h, o, 2))
+                arrived(v_recv(h, o, 3))
 
         def sent(h):
             for n in range(4):
@@ -385,7 +402,7 @@
 
             @pl.when(yl == 0)
             def _():
-                rg[...] = ridge[:, :PANEL]
+                rg[...] = jnp.broadcast_to(ridge[:, :PANEL], (8, PANEL))
                 for d in range(1, 16):
                     r_piece(d).start()
 
@@ -407,10 +424,9 @@
             pltpu.make_async_remote_copy(
                 item, item, zz_s.at[d - 1], zz_r.at[d - 1], device_id=sibling, device_id_type=MESH
             ).wait_recv()
-        steps = plane(zb, 0, 16)
+        steps = plane(zb, 0, 16, lambda item: give(7, item, item).start())
         for step in steps[:-1]:
             step()
-        give_z.start()
 
         for b in range(2):
             rows = zb[b * 2 : b * 2 + 2].reshape(256, K)
@@ -436,7 +452,7 @@
         give_rhs.wait_recv()
         give_top.wait_recv()
         solved = fdot(top[...], inverse[...], across)
-        red[...] = rhs[...] - fdot(solved, panel[...], across)
+        red[...] = (rhs[...] - fdot(solved, panel[...], across))[:1]
         give_red.start()
         keep_red.start()
 
@@ -506,9 +522,20 @@
         trade.start()
         ring(0, 1, 0).start()
         ring(1, 1, 0).start()
-        for n in range(16):
-            at = stage.at[n // 2, :, pl.ds((n % 2) * N, N)]
-            pltpu.make_async_copy(at, at, sc_r.at[n]).wait()
+
+        def staged(gr):
+            for b in range(2):
+                at = stage.at[gr, :, pl.ds(b * N, N)]
+                pltpu.make_async_copy(at, at, sc_r.at[gr * 2 + b]).wait()
+
+        def advance(s, b, way):
+            ring_in(way, s, b).wait_recv()
+            if (s + 1, b, way) in ring_list:
+                ring(way, s + 1, b).start()
+
+        def advance_both(s, b):
+            advance(s, b, 0)
+            advance(s, b, 1)
 
         def s_plane(d):
             to = lax.rem(z + d, NZ)
@@ -517,10 +544,13 @@
                 device_id=dev(x, y, to, 1), device_id_type=MESH,
             )
 
-        for d in (1, 7, 2, 6, 3, 5, 4):
+        for d in (4, 3, 5, 2, 6, 1, 7):
+            staged(lax.rem(z + d, NZ))
             s_plane(d).start()
+        staged(z)
         stay = pltpu.make_async_copy(stage.at[z], sj.at[y, x, :, pair_lanes(z)], lo.at[6])
         stay.start()
+        advance_both(1, 0)
         other = ai.at[z, 1 - yl]
         pltpu.make_async_remote_copy(other, other, ye_s, ye_r, device_id=partner, device_id_type=MESH).wait_recv()
         ring(0, 1, 1).start()
@@ -533,21 +563,21 @@
         stay.wait()
         steps = plane(sj, 1, 32)
 
-        def advance(s, b, way):
-            ring_in(way, s, b).wait_recv()
-            if (s + 1, b, way) in ring_list:
-                ring(way, s + 1, b).start()
-
-        moves = list(ring_list)
-        steps[0]()
-        for step in steps[1:-1]:
-            if len(moves) > 2:
-                advance(*moves.pop(0))
-                advance(*moves.pop(0))
-            step()
-        give_z.wait_recv()
-
-        def group(offsets, fresh):
+        begin, u_first, v_0, u_second, v_1, v_2, v_3, end, ag_sent = steps
+        begin()
+        advance_both(1, 1)
+        u_first()
+        v_0()
+        advance_both(2, 0)
+        u_second()
+        advance_both(2, 1)
+        v_1()
+        v_2()
+        advance_both(3, 0)
+        v_3()
+        advance_both(3, 1)
+
+        def group(offsets, fresh, before_leading, before_columns):
             items = [lax.rem(z + o + NZ, NZ) for o in offsets]
 
             def put(ref, index, value):
@@ -572,8 +602,6 @@
                 put(acc, (rows, slice(None)), total)
                 return c
 
-            lax.fori_loop(0, W // N, split_rows, 0)
-
             def split_leading(n, c):
                 rows = pl.ds(pl.multiple_of(W + n * N, N), N)
                 total = jnp.zeros((N, N), f32)
@@ -587,8 +615,6 @@
                 put(acc, (rows, slice(None)), total)
                 return c
 
-            lax.fori_loop(0, PANEL // N, split_leading, 0)
-
             def left(rows):
                 parts = []
                 for slot in range(4):
@@ -605,8 +631,14 @@
                 put(gi0, (slice(None), part(n)), bdot(left(pl.ds(0, W)), jnp.concatenate(parts, 1), across))
                 return c
 
-            lax.fori_loop(0, PANEL // Q, panel_columns, 0)
-            if not fresh:
+            def sums():
+                ones = jnp.full((8, N), scale, f32)
+                rhs[...] = fdot(ones, acc[:W, :], across)
+                top[...] = fdot(ones, acc[W:, :], across)
+                give_rhs.start()
+                give_top.start()
+
+            def finish_panel():
                 gi0[...] = gi0[...] * scale
                 gi0[:PANEL, :] += diagonal((PANEL, PANEL), 0, ridge[0:1, :PANEL] * on_i)
                 give_gi0.start()
@@ -625,17 +657,20 @@
 
                 return c
 
+            lax.fori_loop(0, W // N, split_rows, 0)
+            before_leading()
+            lax.fori_loop(0, PANEL // N, split_leading, 0)
+            lax.fori_loop(0, PANEL // Q, panel_columns, 0)
+            if not fresh:
+                finish_panel()
+                sums()
+            before_columns()
             lax.fori_loop(0, 4, columns, 0)
 
-        group((0, -1, 1, -2), True)
-        while moves:
-            advance(*moves.pop(0))
-        group((2, -3, 3, 4), False)
-        ones = jnp.full((8, N), scale, f32)
-        rhs[...] = fdot(ones, acc[:W, :], across)
-        top[...] = fdot(ones, acc[W:, :], across)
-        give_rhs.start()
-        give_top.start()
+        group((0, -1, 1, -2), True, give_z.wait_recv, end)
+        advance(4, 0, 0)
+        advance(4, 1, 1)
+        group((2, -3, 3, 4), False, lambda: None, lambda: None)
         give_inverse.wait_recv()
         give_panel.wait_recv()
         keep_panel.start()
@@ -663,22 +698,23 @@
         give_red.wait_recv()
 
     swap.wait_send()
+    swap_targets.wait_send()
 
 
 def on_device(samples, targets, ridge):
-    targets = jnp.broadcast_to(targets[:, None], (targets.shape[0], N))
-    ridge = jnp.broadcast_to(ridge[None, :], (8, ridge.shape[0]))
+    targets, ridge = targets.reshape(1, -1), ridge.reshape(1, -1)
     anywhere = pl.BlockSpec(memory_space=pl.ANY)
     inside = pl.BlockSpec(memory_space=pltpu.VMEM)
     dma = pltpu.SemaphoreType.DMA
-    shapes = [(W, W), (W, PANEL), (8, W)]
+    shapes = [(W, W), (W, PANEL), (1, W)]
     trailing, panel, reduced = pl.pallas_call(
         kernel,
         out_shape=[jax.ShapeDtypeStruct(s, f32) for s in shapes],
         in_specs=[inside] * 3,
         out_specs=[anywhere] * len(shapes),
         scratch_shapes=[
-            pltpu.VMEM((N, W + N), f32),
+            pltpu.VMEM((N, W), f32),
+            pltpu.VMEM((2, 8, N), f32),
             pltpu.VMEM((NZ, 2, W + 8, N), f32),
             pltpu.VMEM((4, 4, 64, K), f32),
             pltpu.VMEM((4, 4, 32, K), f32),
@@ -696,8 +732,8 @@
             pltpu.VMEM((W, PANEL), f32),
             pltpu.VMEM((8, W), f32),
             pltpu.VMEM((8, PANEL), f32),
-            pltpu.VMEM((8, W), f32),
-            dma, dma, dma, dma,
+            pltpu.VMEM((1, W), f32),
+            dma((2,)), dma((2,)), dma, dma,
             dma((2, 4, 2)), dma((2, 4, 2)),
             dma((16,)), dma((16,)),
             dma((16,)), dma((2,)),
@@ -711,7 +747,7 @@
         ),
         name="ridge_panel",
     )(samples, targets, ridge)
-    return trailing, panel, reduced[0]
+    return trailing, panel, reduced.reshape(-1)
 
 
 def solution(mesh):

time: 121 us -> 111 us (0.917)
  Pallas kernels: 110 us -> 104 us
  local copies, waits for them, and re-layouts: 10.3 us -> 6.86 us
    pallas_call x1, Pallas kernels: 110 us -> 104 us  [on_device(): pl.pallas_call(kernel, out_shape=[jax.ShapeDtypeStruct(s, f32) for s in s...]
    broadcast_in_dim x2 -> x0, local copies, waits for them, and re-layouts: 2.65 us -> none  [the longest x1 1.34 us: on_device(): targets = jnp.broadcast_to(targets[:, None], (targets.shape[0], N))]
    slice x1 -> x0, local copies, waits for them, and re-layouts: 1.35 us -> none  [on_device(): return (trailing, panel, reduced[0])]
    unnamed x4 -> x7, local copies, waits for them, and re-layouts: 6.26 us -> 6.86 us
where the time goes in v3:
time: 111 us
  Pallas kernels  104 us (94%)
  local copies, waits for them, and re-layouts  6.86 us (6%)
    pallas_call x1, Pallas kernels, on_device(): pl.pallas_call(kernel, out_shape=[jax.ShapeDtypeStruct(s, f32) for s in s...  104 us
    unnamed x7, local copies, waits for them, and re-layouts  6.86 us

profile of v3, /device:TPU:1, one launch (start us, length us, event | category | flops | bytes accessed | tf_op | source)
XLA Modules:
  0.0 111.2 jit_solution(167400999560448857)
XLA Ops:
  0.6 103.7 %ridge_panel.1 = (f32[1024,1024]{1,0:T(8,128)}, f32[1024,512]{1,0:T(8,128)}, f32[1,1024]{1,0:T(1,128)}) custom-call(f32[64,1024]{1,0:T(8,128)} %samp.1, f32[1,64]{1,0:T(1,128)} %bitcast.5, f32[1,1024]{1,0:T(1,128)} %bitcast.3), custom_call_target="tpu_custom_call" | custom-call | tf_op jit(solution)/shard_map/ridge_panel/pallas_call | solution.py:710
  104.4 0.0 copy-start
  104.4 0.0 copy-start.1
  104.4 4.9 %copy.9 = f32[1024,1024]{1,0:T(8,128)} copy(f32[1024,1024]{1,0:T(8,128)} %get-tuple-element.12) | data formatting | bytes 8388608
  109.3 0.0 copy-done
  109.3 1.3 %copy.10 = f32[1024,512]{1,0:T(8,128)} copy(f32[1024,512]{1,0:T(8,128)S(1)} %copy-done) | data formatting | bytes 4194304
  110.6 0.0 copy-done.1
  110.6 0.6 copy.11
Async XLA Ops:
  104.4 5.0 %copy-start = (f32[1024,512]{1,0:T(8,128)S(1)}, f32[1024,512]{1,0:T(8,128)}, u32[]{:S(2)}) copy-start(f32[1024,512]{1,0:T(8,128)} %get-tuple-element.13) | copy-start | bytes 6291460
  104.4 6.3 %copy-start.1 = (f32[1,1024]{1,0:T(1,128)S(1)}, f32[1,1024]{1,0:T(1,128)}, u32[]{:S(2)}) copy-start(f32[1,1024]{1,0:T(1,128)} %get-tuple-element.8) | copy-start | bytes 12292

commit v4 on v3

--- a/solution.py
+++ b/solution.py
@@ -141,7 +141,7 @@
 def kernel(
     samp, targ, ridge,
     out_o, panel_o, red_o,
-    chunk, tr, ai, sj, zb, stage, rg, azh, azl, tg, gi0, acc, g00, inverse, ab, mm, panel, rhs, top, red,
+    chunk, tr, ai, sj, zb, stage, rg, azh, azl, tg, gi0, acc, g00, inverse, ab, mm, panel, red,
     ex_s, ex_r, ye_s, ye_r, si_s, si_r, sc_s, sc_r, zs_s, zs_r, rg_s, rg_r, zz_s, zz_r, ag_s, ag_r, h_s, h_r, lo,
 ):
     r, i, z = lax.axis_index("rows"), lax.axis_index("gr"), lax.axis_index("gc")
@@ -338,8 +338,7 @@
         return pl.ds(pl.multiple_of(n * Q, Q), Q)
 
     give_gi0 = give(0, gi0, gi0)
-    give_rhs = give(1, rhs, rhs)
-    give_top = give(2, top, top)
+    give_acc = give(1, acc, acc)
     give_z = give(7, zb, zb)
     give_inverse = give(8, inverse, inverse)
     give_panel = give(9, panel, panel)
@@ -446,15 +445,16 @@
             panel[rows, :] = dot3(gi0[rows, :], inverse[...], across)
         give_panel.start()
         keep_panel.start()
+        give_acc.wait_recv()
+        ones = jnp.full((8, N), scale, f32)
+        rhs = fdot(ones, acc[:W, :], across)
+        top = fdot(ones, acc[W:, :], across)
+        red[...] = (rhs - fdot(fdot(top, inverse[...], across), panel[...], across))[:1]
+        give_red.start()
+        keep_red.start()
         for n in range(NS):
             give_tile(n).wait_recv()
             update(n)
-        give_rhs.wait_recv()
-        give_top.wait_recv()
-        solved = fdot(top[...], inverse[...], across)
-        red[...] = (rhs[...] - fdot(solved, panel[...], across))[:1]
-        give_red.start()
-        keep_red.start()
 
         steps[-1]()
         for d in range(1, NZ):
@@ -631,14 +631,8 @@
                 put(gi0, (slice(None), part(n)), bdot(left(pl.ds(0, W)), jnp.concatenate(parts, 1), across))
                 return c
 
-            def sums():
-                ones = jnp.full((8, N), scale, f32)
-                rhs[...] = fdot(ones, acc[:W, :], across)
-                top[...] = fdot(ones, acc[W:, :], across)
-                give_rhs.start()
-                give_top.start()
-
             def finish_panel():
+                give_acc.start()
                 gi0[...] = gi0[...] * scale
                 gi0[:PANEL, :] += diagonal((PANEL, PANEL), 0, ridge[0:1, :PANEL] * on_i)
                 give_gi0.start()
@@ -663,7 +657,6 @@
             lax.fori_loop(0, PANEL // Q, panel_columns, 0)
             if not fresh:
                 finish_panel()
-                sums()
             before_columns()
             lax.fori_loop(0, 4, columns, 0)
 
@@ -686,8 +679,7 @@
         for d in range(1, NZ):
             s_plane(d).wait_send()
         give_gi0.wait_send()
-        give_rhs.wait_send()
-        give_top.wait_send()
+        give_acc.wait_send()
         keep_panel.wait()
         for n in range(NS):
             give_tile(n).wait_send()
@@ -699,6 +691,22 @@
 
     swap.wait_send()
     swap_targets.wait_send()
+
+
+def hand_out(trailing, panel):
+    def copy(t_ref, p_ref, t_out, p_out):
+        t_out[...] = t_ref[...]
+        p_out[...] = p_ref[...]
+
+    specs = [pl.BlockSpec((Q, W), lambda n: (n, 0)), pl.BlockSpec((Q, PANEL), lambda n: (n, 0))]
+    return pl.pallas_call(
+        copy,
+        grid=(W // Q,),
+        out_shape=[jax.ShapeDtypeStruct((W, W), f32), jax.ShapeDtypeStruct((W, PANEL), f32)],
+        in_specs=specs,
+        out_specs=specs,
+        name="hand_out",
+    )(trailing, panel)
 
 
 def on_device(samples, targets, ridge):
@@ -730,8 +738,6 @@
             pltpu.VMEM((N, 2 * N), f32),
             pltpu.VMEM((N, N), f32),
             pltpu.VMEM((W, PANEL), f32),
-            pltpu.VMEM((8, W), f32),
-            pltpu.VMEM((8, PANEL), f32),
             pltpu.VMEM((1, W), f32),
             dma((2,)), dma((2,)), dma, dma,
             dma((2, 4, 2)), dma((2, 4, 2)),
@@ -747,6 +753,7 @@
         ),
         name="ridge_panel",
     )(samples, targets, ridge)
+    trailing, panel = hand_out(trailing, panel)
     return trailing, panel, reduced.reshape(-1)
 
 

time: 111 us -> 110 us (level)
  local copies, waits for them, and re-layouts: 6.86 us -> 0.6 us
  Pallas kernels: 104 us -> 109 us
    unnamed x7 -> x3, local copies, waits for them, and re-layouts: 6.86 us -> 0.6 us
    pallas_call x0 -> x1, Pallas kernels: none -> 5.83 us  [hand_out(): pl.pallas_call(copy, grid=(W // Q,), out_shape=[jax.ShapeDtypeStruct((W,...]
where the time goes in v4:
time: 110 us
  Pallas kernels  109 us (99%)
    pallas_call x1, Pallas kernels, on_device(): pl.pallas_call(kernel, out_shape=[jax.ShapeDtypeStruct(s, f32) for s in s...  103 us
    pallas_call x1, Pallas kernels, hand_out(): pl.pallas_call(copy, grid=(W // Q,), out_shape=[jax.ShapeDtypeStruct((W,...  5.83 us

profile of v4, /device:TPU:1, one launch (start us, length us, event | category | flops | bytes accessed | tf_op | source)
XLA Modules:
  0.0 110.1 jit_solution(12534130744101360291)
XLA Ops:
  0.6 103.0 %ridge_panel.1 = (f32[1024,1024]{1,0:T(8,128)}, f32[1024,512]{1,0:T(8,128)}, f32[1,1024]{1,0:T(1,128)}) custom-call(f32[64,1024]{1,0:T(8,128)} %samp.1, f32[1,64]{1,0:T(1,128)} %bitcast.5, f32[1,1024]{1,0:T(1,128)} %bitcast.3), custom_call_target="tpu_custom_call" | custom-call | tf_op jit(solution)/shard_map/ridge_panel/pallas_call | solution.py:718
  103.6 0.0 copy-start
  103.6 5.8 %hand_out.1 = (f32[1024,1024]{1,0:T(8,128)}, f32[1024,512]{1,0:T(8,128)}) custom-call(f32[1024,1024]{1,0:T(8,128)} %get-tuple-element.8.t_ref, f32[1024,512]{1,0:T(8,128)} %get-tuple-element.9.p_ref), custom_call_target="tpu_custom_call" | custom-call | tf_op jit(solution)/shard_map/hand_out/pallas_call | solution.py:702
  109.5 0.0 copy-done
  109.5 0.6 copy.7
Async XLA Ops:
  103.6 5.8 %copy-start = (f32[1,1024]{1,0:T(1,128)S(1)}, f32[1,1024]{1,0:T(1,128)}, u32[]{:S(2)}) copy-start(f32[1,1024]{1,0:T(1,128)} %get-tuple-element.12) | copy-start | bytes 12292
